TPU v7x, 256 devices: a whole 4x4x8 slice. The times are simulated.
256 devices in a mesh: dp: 8 (over y, core), table: 32 (over x, z).
Axes of the slice: x: 4, y: 4, z: 8, core: 2. Of those that a mesh axis runs over, the one named last changes fastest.
Arguments:
- embed_table: bfloat16 [65536, 512], P('table'), may hold values from -6 to 6
- owner_shard: int32 [2048, 64, 2, 1], P(('dp', 'table')), may hold values from 0 to 31; in each aligned block of 128 rows (0 to 127, 128 to 255, ..., all dimensions but the last counted through in order) at most 8 rows name the same one
- slot_row: int32 [2048, 64, 2], P(('dp', 'table')), may hold values from 0 to 2047
- lengths: int32 [2048], P(('dp', 'table')), may hold values from 1 to 64, as said below
- send_order: int32 [256, 8], P(('dp', 'table')), may hold values from 0 to 7, each once within a row
- proj_weight: bfloat16 [1024, 3072], replicated, may hold values from -0.1875 to 0.1875
- out_weight: bfloat16 [1024, 1024], replicated, may hold values from -0.1875 to 0.1875
- upstream: bfloat16 [2048, 64, 1024], P(('dp', 'table')), may hold values from -6 to 6
Outputs:
- table_grad: bfloat16 [65536, 512], P('table', 'dp')
- proj_grad: bfloat16 [1024, 3072], P('table', 'dp')
- out_grad: bfloat16 [1024, 1024], P('table', 'dp')
Inputs may be any that keep to these rules, and one draw needn't show every extreme that they name: `owner_shard`: within the 128 lookups of one history no owner shard is named more than 8 times. `lengths`: every device has at least one history of all 64 positions. `send_order`: each row is a permutation.
All inputs are finite; a program needn't handle non-finite values.
Results may differ from a plain program's by a relative error of at most 0.029.
Values may be sent and summed in bfloat16 or wider, within the bound.
A program may use at most 128 MiB of HBM per device.

v0:
```python
import jax
import jax.numpy as jnp
from jax import lax
from jax.sharding import PartitionSpec as P

D = 1024
HEADS = 8
QK = 64


EPSILON = 1e-06


def norm_rows(values):
    average = jnp.mean(values, axis=-1, keepdims=True)
    centred = values - average
    spread = jnp.mean(centred * centred, axis=-1, keepdims=True)
    return centred * lax.rsqrt(spread + EPSILON)


def attend(projected, lengths):
    blocks, positions, _ = projected.shape
    value_width = D
    query_width = HEADS * QK
    gate_part = projected[:, :, :value_width].astype(jnp.float32)
    values = projected[:, :, value_width : 2 * value_width].reshape(
        blocks, positions, HEADS, value_width // HEADS
    )
    queries = projected[:, :, 2 * value_width : 2 * value_width + query_width].reshape(
        blocks, positions, HEADS, QK
    )
    key_part = projected[:, :, 2 * value_width + query_width :].reshape(
        blocks, positions, HEADS, QK
    )
    scores = jnp.einsum("bqhd,bkhd->bhqk", queries, key_part, preferred_element_type=jnp.float32)
    places = jnp.arange(positions)
    causal = places[:, None] >= places[None, :]
    weights = (
        jnp.where(causal[None, None], jax.nn.silu(scores), 0.0)
        / lengths.astype(jnp.float32)[:, None, None, None]
    )
    weights = weights.astype(jnp.bfloat16)
    attended = jnp.einsum("bhqk,bkhd->bqhd", weights, values, preferred_element_type=jnp.float32)
    return norm_rows(attended.reshape(blocks, positions, value_width)) * gate_part


def local_layer(fetched, lengths, upstream, proj_weight, out_weight):
    blocks, positions, feature_count = fetched.shape
    is_valid = jnp.arange(positions)[None, :] < lengths[:, None]
    grad_top = jnp.where(is_valid[:, :, None], upstream, jnp.zeros_like(upstream))
    flat_rows = fetched.reshape(blocks * positions, feature_count).astype(jnp.float32)
    normed_full, norm_back = jax.vjp(norm_rows, flat_rows)
    normed = normed_full.astype(jnp.bfloat16)
    before = jnp.dot(normed, proj_weight, preferred_element_type=jnp.float32)
    projected = jax.nn.silu(before).astype(jnp.bfloat16).reshape(blocks, positions, -1)
    mixed_full, attend_back = jax.vjp(lambda inner: attend(inner, lengths), projected)
    mixed = mixed_full.astype(jnp.bfloat16).reshape(blocks * positions, -1)
    flat_top = grad_top.reshape(blocks * positions, -1)
    grad_mixed = lax.dot_general(
        flat_top, out_weight, (((1,), (1,)), ((), ())), preferred_element_type=jnp.float32
    ).astype(jnp.bfloat16)
    grad_projected = attend_back(grad_mixed.reshape(blocks, positions, -1).astype(jnp.float32))[0]
    sigmoid_before = jax.nn.sigmoid(before)
    slope = sigmoid_before * (1.0 + before * (1.0 - sigmoid_before))
    grad_before = (
        grad_projected.reshape(blocks * positions, -1).astype(jnp.float32) * slope
    ).astype(jnp.bfloat16)
    grad_normed = lax.dot_general(
        grad_before, proj_weight, (((1,), (1,)), ((), ())), preferred_element_type=jnp.float32
    )
    grad_rows = (norm_back(grad_normed)[0] + flat_top.astype(jnp.float32)).astype(jnp.bfloat16)
    return (
        normed,
        mixed,
        flat_top,
        grad_before,
        grad_rows.reshape(blocks, positions, feature_count),
    )


def fetch_rows(embed_table, owner_part, row_part, shard_count, capacity):
    owners = owner_part.reshape(-1)
    wanted = row_part.reshape(-1)
    chosen = (owners[:, None] == jnp.arange(shard_count)[None, :]).astype(jnp.int32)
    ranked = jnp.sum(jnp.cumsum(chosen, axis=0) * chosen, axis=1) - 1
    slot_index = owners * capacity + ranked
    request = jnp.full((shard_count * capacity,), -1, jnp.int32).at[slot_index].set(wanted)
    request = request.reshape(shard_count, capacity)
    requested = lax.all_to_all(request, "table", split_axis=0, concat_axis=0, tiled=True)
    present = requested >= 0
    picked = jnp.take(embed_table, jnp.maximum(requested, 0), axis=0)
    picked = jnp.where(present[:, :, None], picked, jnp.zeros_like(picked))
    returned = lax.all_to_all(picked, "table", split_axis=0, concat_axis=0, tiled=True)
    replies, requested = (returned, requested)
    fetched = replies.reshape(shard_count * capacity, -1)[slot_index]
    return (fetched.reshape(owner_part.shape[0], owner_part.shape[1], -1), slot_index, requested)


def give_back(grad_rows, slot_index, requested, shard_count, capacity, row_count, emb_width):
    flat = grad_rows.reshape(-1, emb_width)
    outgoing = jnp.zeros((shard_count * capacity, emb_width), jnp.bfloat16).at[slot_index].set(flat)
    incoming = lax.all_to_all(
        outgoing.reshape(shard_count, capacity, emb_width),
        "table",
        split_axis=0,
        concat_axis=0,
        tiled=True,
    )
    asked_flat = requested.reshape(-1)
    present = asked_flat >= 0
    contrib = jnp.where(present[:, None], incoming.reshape(-1, emb_width).astype(jnp.float32), 0.0)
    return (
        jnp.zeros((row_count, emb_width), jnp.float32).at[jnp.maximum(asked_flat, 0)].add(contrib)
    )


def body(
    embed_table, owner_shard, slot_row, lengths, send_order, proj_weight, out_weight, upstream
):
    hist_count = slot_row.shape[0]
    positions = slot_row.shape[1]
    shard_count = lax.axis_size("table")
    group_count = lax.axis_size("dp")
    capacity = hist_count * (4 * positions // shard_count)
    hand_order = send_order[0]
    owner_sorted = owner_shard[hand_order]
    row_sorted = slot_row[hand_order]
    length_sorted = lengths[hand_order]
    fetched, slot_index, requested = fetch_rows(
        embed_table, owner_sorted, row_sorted, shard_count, capacity
    )
    moved, arrived = (
        lax.all_to_all(fetched, "dp", split_axis=0, concat_axis=0, tiled=True),
        lax.all_to_all(length_sorted, "dp", split_axis=0, concat_axis=0, tiled=True),
    )
    normed, mixed, flat_top, grad_before, grad_rows = local_layer(
        moved, arrived, upstream, proj_weight, out_weight
    )
    returned = lax.all_to_all(grad_rows, "dp", split_axis=0, concat_axis=0, tiled=True)
    table_sum = give_back(
        returned,
        slot_index,
        requested,
        shard_count,
        capacity,
        embed_table.shape[0],
        embed_table.shape[1],
    )
    grad_scale = float(hist_count * positions * group_count * shard_count) ** (-0.5)
    count = lax.axis_size("table") * (normed.shape[1] // shard_count)
    first = (
        lax.dot_general(
            normed, grad_before, (((0,), (0,)), ((), ())), preferred_element_type=jnp.float32
        )
        * grad_scale
    )
    second = (
        lax.dot_general(
            mixed, flat_top, (((0,), (0,)), ((), ())), preferred_element_type=jnp.float32
        )
        * grad_scale
    )
    first = first.reshape(count, group_count, -1)
    second = second.reshape(count, group_count, -1)
    share = lax.psum_scatter(
        jnp.concatenate([first, second], axis=2).reshape(count, -1).astype(jnp.bfloat16),
        "table",
        scatter_dimension=0,
        tiled=True,
    )
    dense_sum, table_part = (
        lax.psum_scatter(share, "dp", scatter_dimension=1, tiled=True).astype(jnp.float32),
        lax.psum_scatter(
            table_sum.astype(jnp.bfloat16), "dp", scatter_dimension=1, tiled=True
        ).astype(jnp.float32),
    )
    split_at = proj_weight.shape[1] // group_count
    return (
        table_part.astype(jnp.bfloat16),
        dense_sum[:, :split_at].astype(jnp.bfloat16),
        dense_sum[:, split_at:].astype(jnp.bfloat16),
    )


def solution(mesh):
    in_specs = (
        P("table", None),
        P(("dp", "table"), None, None, None),
        P(("dp", "table"), None, None),
        P(("dp", "table")),
        P(("dp", "table"), None),
        P(),
        P(),
        P(("dp", "table"), None, None),
    )
    out_specs = (P("table", "dp"), P("table", "dp"), P("table", "dp"))
    return jax.shard_map(body, mesh=mesh, in_specs=in_specs, out_specs=out_specs, check_vma=False)
```

profile of v0, /device:TPU:1, one launch (start us, length us, event | category | flops | bytes accessed | tf_op | source)
XLA Modules:
  0.0 541.2 jit_solution(3334968660842352716)
XLA Ops:
  10.9 9.0 %reduce-window.6 = s32[32,8,128]{2,1,0:T(8,128)S(1)} reduce-window(s32[32,8,128]{2,1,0:T(8,128)S(1)} %fusion.37, s32[]{:T(128)} %constant.26.clone.1), window={size=1x1x128 pad=0_0x0_0x127_0}, to_apply=%region_0.0 | reduce-window | flops 4161536 | bytes 262148 | tf_op jit(solution)/shard_map/reduce-window
  21.3 4.3 scatter_custom_fusion
  25.7 20.3 %all_to_all.38 = s32[32,1,64]{2,1,0:T(1,128)S(1)} all-to-all(s32[32,1,64]{2,1,0:T(1,128)S(1)} %all_to_all.24), channel_id=1, replica_groups=mesh['dp'=8,'table'=32] {'table'}, dimensions={0} | all-to-all | bytes 16384 | tf_op jit(solution)/shard_map/all_to_all | solution.py:89
  46.1 9.2 %gather_fusion.3 = bf16[2048,512]{1,0:T(8,128)(2,1)} fusion(bf16[2048,512]{1,0:T(8,128)(2,1)S(1)} %copy-done, s32[2048]{0:T(1024)S(1)} %broadcast_clamp_fusion), kind=kCustom, calls=%fused_computation.3 | custom fusion | bytes 4202496 | tf_op jit(solution)/shard_map/jit(_take)/gather | solution.py:91
  55.3 2.9 select_select_fusion
  58.2 4.1 all-to-all-start.2
  63.7 48.0 %all-to-all-done.2 = bf16[32,64,512]{2,1,0:T(8,128)(2,1)S(1)} async-done(((bf16[32,64,512]{2,1,0:T(8,128)(2,1)}), bf16[32,64,512]{2,1,0:T(8,128)(2,1)S(1)}, u32[]{:S(2)}, u32[]{:S(2)}) %all-to-all-start.2) | async-done | bytes 2097184 | tf_op jit(solution)/shard_map/all_to_all | solution.py:93
  111.7 6.4 %all-to-all-start.1 = ((s32[8,1,1]{2,1,0:T(1,128)}), s32[8,1,1]{2,1,0:T(1,128)S(1)}, u32[]{:S(2)}, u32[]{:S(2)}) async-start(s32[8,1,1]{2,1,0:T(1,128)} %copy.120), calls=%async_computation.1 | async-start | bytes 8192 | tf_op jit(solution)/shard_map/all_to_all | solution.py:134
  118.1 4.0 gather_fusion.4
  123.2 4.8 all-to-all-start.3
  131.6 11.6 %all-to-all-done.3 = bf16[8,64,1024]{2,1,0:T(8,128)(2,1)S(1)} async-done(((bf16[8,64,1024]{2,1,0:T(8,128)(2,1)}), bf16[8,64,1024]{2,1,0:T(8,128)(2,1)S(1)}, u32[]{:S(2)}, u32[]{:S(2)}) %all-to-all-start.3) | async-done | bytes 1048608 | tf_op jit(solution)/shard_map/all_to_all | solution.py:133
  144.3 8.7 %multiply_convert_fusion.1 = (bf16[512,3072]{1,0:T(8,128)(2,1)S(1)}, f32[512,3072]{1,0:T(8,128)}) fusion(bf16[512,1024]{1,0:T(8,128)(2,1)S(1)} %multiply_convert_fusion.2, bf16[1024,3072]{1,0:T(8,128)(2,1)} %param.13), kind=kOutput, calls=%fused_computation.12 | convolution fusion | flops 3229089792 | bytes 16777216 | tf_op jit(solution)/shard_map/dot_general | solution.py:54
  157.4 2.4 reshape.330
  164.2 2.9 fusion.1
  175.8 4.6 copy.134
  182.3 2.6 reshape.333
  188.6 4.5 fusion
  193.2 3.7 multiply_convert_fusion
  196.9 4.3 copy.145
  201.2 6.8 %pad_maximum_fusion = bf16[1024,8,512]{2,1,0:T(8,128)(2,1)} fusion(bf16[1024,8,128]{2,1,0:T(8,128)(2,1)S(1)} %copy-done.5, bf16[1024,8,384]{2,1,0:T(8,128)(2,1)} %bitcast.175), kind=kLoop, calls=%fused_computation.9 | loop fusion | flops 16777216 | bytes 16777216 | tf_op jit(solution)/shard_map/concatenate | solution.py:166
  208.0 12.2 %copy.146 = bf16[128,8,8,512]{3,1,2,0:T(8,128)(2,1)} copy(bf16[128,8,8,512]{3,2,1,0:T(8,128)(2,1)} %bitcast.174) | data formatting | bytes 16777216
  220.2 6.7 %multiply_reduce_fusion = (f32[512]{0:T(512)S(1)}, f32[512,1024]{1,0:T(8,128)S(1)}) fusion(bf16[8,64,1024]{2,1,0:T(8,128)(2,1)S(1)} %all-to-all-done.3, f32[512]{0:T(512)S(1)} %div.62, bf16[512,3072]{1,0:T(8,128)(2,1)} %copy-done.13, bf16[1024,3072]{1,0:T(8,128)(2,1)} %param.13), kind=kOutput, calls=%fused_computation.38 | convolution fusion | flops 3223322112 | bytes 12587008 | tf_op jit(solution)/shard_map/dot_general | solution.py:68
  228.9 18.5 %all_to_all.39 = bf16[8,64,1024]{2,1,0:T(8,128)(2,1)S(1)} all-to-all(bf16[8,64,1024]{2,1,0:T(8,128)(2,1)S(1)} %bitcast.190), channel_id=1, replica_groups=mesh['dp'=8,'table'=32] {'dp'}, dimensions={0} | all-to-all | bytes 2097152 | tf_op jit(solution)/shard_map/all_to_all | solution.py:139
  247.8 6.7 %scatter_custom_fusion.1 = bf16[2048,512]{1,0:T(8,128)(2,1)} fusion(s32[1024]{0:T(1024)S(1)} %bitcast.202, bf16[1024,512]{1,0:T(8,128)(2,1)S(1)} %reshape.399, bf16[]{:T(256)} %constant.31.clone.1), kind=kCustom, calls=%fused_computation.66 | custom fusion | bytes 2097154 | tf_op jit(solution)/shard_map/scatter | solution.py:101
  254.6 5.6 %all-to-all-start.5 = ((bf16[32,64,512]{2,1,0:T(8,128)(2,1)}), bf16[32,64,512]{2,1,0:T(8,128)(2,1)S(1)}, u32[]{:S(2)}, u32[]{:S(2)}) async-start(bf16[32,64,512]{2,1,0:T(8,128)(2,1)} %bitcast.186), calls=%async_computation.5 | async-start | bytes 4194304 | tf_op jit(solution)/shard_map/all_to_all | solution.py:102
  260.3 200.7 %reduce-scatter.6.cloned.1.call-done = bf16[32,4096]{1,0:T(8,128)(2,1)} async-done(((bf16[1024,4096]{1,0:T(8,128)(2,1)}), bf16[32,4096]{1,0:T(8,128)(2,1)}) %reduce-scatter.6.cloned.1.call-update) | async-done | bytes 262160 | tf_op jit(solution)/shard_map/reduce_scatter | solution.py:165
  461.0 2.4 convert_select_fusion
  463.4 16.6 %scatter_custom_fusion.2 = f32[2048,512]{1,0:T(8,128)} fusion(s32[2048]{0:T(1024)S(1)} %reshape.405, f32[2048,512]{1,0:T(8,128)} %convert_select_fusion, f32[]{:T(128)} %constant.24.clone.1), kind=kCustom, calls=%fused_computation.46 | custom fusion | flops 1048576 | bytes 4194816 | tf_op jit(solution)/shard_map/scatter-add | solution.py:113
  480.0 3.8 convert_element_type.134
  483.8 4.1 copy.138
  488.0 8.7 %reduce-scatter.8.cloned.1.call-done = bf16[32,512]{1,0:T(8,128)(2,1)} async-done(((bf16[32,4096]{1,0:T(8,128)(2,1)}), bf16[32,512]{1,0:T(8,128)(2,1)}) %reduce-scatter.8.cloned.1.call-update) | async-done | bytes 32784 | tf_op jit(solution)/shard_map/reduce_scatter | solution.py:172
  499.4 35.2 %reduce-scatter.10.cloned.1.call-done = bf16[64,2048]{1,0:T(8,128)(2,1)} async-done(((bf16[512,2048]{1,0:T(8,128)(2,1)}), bf16[64,2048]{1,0:T(8,128)(2,1)}) %reduce-scatter.10.cloned.1.call-update) | async-done | bytes 262160
  (118 shorter events, 40.5 us)
Async XLA Ops:
  7.2 38.9 %copy-start = (bf16[2048,512]{1,0:T(8,128)(2,1)S(1)}, bf16[2048,512]{1,0:T(8,128)(2,1)}, u32[]{:S(2)}) copy-start(bf16[2048,512]{1,0:T(8,128)(2,1)} %param.8) | copy-start | bytes 6291460
  58.2 4.2 copy-start.2
  58.2 53.5 %all-to-all-start.2 = ((bf16[32,64,512]{2,1,0:T(8,128)(2,1)}), bf16[32,64,512]{2,1,0:T(8,128)(2,1)S(1)}, u32[]{:S(2)}, u32[]{:S(2)}) async-start(bf16[32,64,512]{2,1,0:T(8,128)(2,1)} %select_select_fusion), calls=%async_computation.2 | async-start | bytes 4194304 | tf_op jit(solution)/shard_map/all_to_all | solution.py:93
  111.7 11.5 %all-to-all-start.1 = ((s32[8,1,1]{2,1,0:T(1,128)}), s32[8,1,1]{2,1,0:T(1,128)S(1)}, u32[]{:S(2)}, u32[]{:S(2)}) async-start(s32[8,1,1]{2,1,0:T(1,128)} %copy.120), calls=%async_computation.1 | async-start | bytes 8192 | tf_op jit(solution)/shard_map/all_to_all | solution.py:134
  122.0 6.4 %copy-start.16 = (bf16[8,64,1024]{2,1,0:T(8,128)(2,1)S(1)}, bf16[8,64,1024]{2,1,0:T(8,128)(2,1)}, u32[]{:S(2)}) copy-start(bf16[8,64,1024]{2,1,0:T(8,128)(2,1)} %param.15) | copy-start | bytes 3145732
  123.2 19.9 %all-to-all-start.3 = ((bf16[8,64,1024]{2,1,0:T(8,128)(2,1)}), bf16[8,64,1024]{2,1,0:T(8,128)(2,1)S(1)}, u32[]{:S(2)}, u32[]{:S(2)}) async-start(bf16[8,64,1024]{2,1,0:T(8,128)(2,1)} %reshape.326), calls=%async_computation.3 | async-start | bytes 2097152 | tf_op jit(solution)/shard_map/all_to_all | solution.py:133
  128.0 332.9 %reduce-scatter.6.cloned.1.call-start = ((), (), s32[]{:S(2)}) async-start(), calls=%async_computation.9 | async-start | bytes 8650752 | tf_op jit(solution)/shard_map/reduce_scatter | solution.py:165
  128.3 2.0 copy-start.17
  128.5 1.0 copy-start.9
  144.3 8.7 %copy-start.14 = (bf16[512,1024]{1,0:T(8,128)(2,1)}, bf16[512,1024]{1,0:T(8,128)(2,1)S(1)}, u32[]{:S(2)}) copy-start(bf16[512,1024]{1,0:T(8,128)(2,1)S(1)} %multiply_convert_fusion.2) | copy-start | bytes 3145732
  152.9 1.7 copy-start.3
  159.8 2.3 copy-start.4
  163.0 1.2 copy-start.10
  170.3 1.2 copy-start.6
  175.8 4.6 copy-start.8
  180.5 4.4 copy-start.7
  185.5 1.4 copy-start.12
  188.6 4.5 copy-start.15
  193.2 3.7 copy-start.13
  196.9 4.3 copy-start.5
  226.9 1.2 copy-start.11
  254.6 206.4 %all-to-all-start.5 = ((bf16[32,64,512]{2,1,0:T(8,128)(2,1)}), bf16[32,64,512]{2,1,0:T(8,128)(2,1)S(1)}, u32[]{:S(2)}, u32[]{:S(2)}) async-start(bf16[32,64,512]{2,1,0:T(8,128)(2,1)} %bitcast.186), calls=%async_computation.5 | async-start | bytes 4194304 | tf_op jit(solution)/shard_map/all_to_all | solution.py:102
  260.1 236.6 %reduce-scatter.8.cloned.1.call-start = ((), (), s32[]{:S(2)}) async-start(), calls=%async_computation.10 | async-start | bytes 294912 | tf_op jit(solution)/shard_map/reduce_scatter | solution.py:172
  460.9 73.6 %reduce-scatter.10.cloned.1.call-start = ((), (), s32[]{:S(2)}) async-start(), calls=%async_computation.11 | async-start | bytes 2359296
  483.8 50.7 %copy-start.1 = (bf16[2048,512]{1,0:T(8,128)(2,1)S(1)}, bf16[2048,512]{1,0:T(8,128)(2,1)}, u32[]{:S(2)}) copy-start(bf16[2048,512]{1,0:T(8,128)(2,1)} %param.8) | copy-start | bytes 6291460
Sparse Core Ops, SparseCore 0:
  220.3 240.5 reduce-scatter.5
  463.6 33.0 reduce-scatter.7
  499.8 34.6 reduce-scatter.9
where the time goes:
time: 550 us; the launch traced here: 541 us
  waiting for transfers between devices  304 us (55%)
  local copies, waits for them, and re-layouts  77 us (14%)
  other arithmetic  55.2 us (10%)
  blocking collectives  38.8 us (7%)
  matrix products  30.5 us (6%)
  starting transfers between devices  21 us (4%)
  between operations  14.4 us (3%)
    reduce_scatter x1, waiting for transfers between devices, body(): lax.psum_scatter(jnp.concatenate([first, second], axis=2).reshape(count,...  201 us
    all_to_all x1, waiting for transfers between devices, fetch_rows(): lax.all_to_all(picked, 'table', split_axis=0, concat_axis=0, tiled=True)  48 us
    unnamed x4, waiting for transfers between devices  35.2 us
    unnamed x39, local copies, waits for them, and re-layouts  25.4 us
    all_to_all x1, blocking collectives, fetch_rows(): lax.all_to_all(request, 'table', split_axis=0, concat_axis=0, tiled=True)  20.3 us
    all_to_all x1, blocking collectives, body(): lax.all_to_all(grad_rows, 'dp', split_axis=0, concat_axis=0, tiled=True)  18.5 us
    scatter-add x1, other arithmetic, give_back(): jnp.zeros((row_count, emb_width), jnp.float32)  16.6 us
    all_to_all x1, waiting for transfers between devices, body(): lax.all_to_all(fetched, 'dp', split_axis=0, concat_axis=0, tiled=True)  11.6 us
  transfers between devices with their start and end apart: 7, of which 5 were waited for; matrix products, arithmetic and copies ran while one was open for 10% of the time, Pallas kernels for 0%

commit v1 on v0

v1 whole, which is shorter than its diff:
```python
import functools

import jax
import jax.numpy as jnp
from jax import lax
from jax.experimental import pallas as pl
from jax.experimental.pallas import tpu as pltpu
from jax.sharding import PartitionSpec as P

D = 1024
EMB = 512
HEADS = 8
QK = 64
PROJ = 3072
SEQ = 64
HIST = 8
ROWS_DEV = 2048
MOST = 8
N_DP = 8
N_TABLE = 32
PAIRS = HIST // 2
TOK = 2 * SEQ
SLOTS = 2 * N_TABLE * MOST
EPSILON = 1e-06
SCALE = float(2048 * 64) ** (-0.5)
MESH = pl.DeviceIdType.MESH
VMEM_LIMIT = 60 * 1024 * 1024
F32 = jnp.float32
BF16 = jnp.bfloat16


def mm(a, b):
    return lax.dot_general(a, b, (((1,), (0,)), ((), ())), preferred_element_type=F32)


def mm_nt(a, b):
    return lax.dot_general(a, b, (((1,), (1,)), ((), ())), preferred_element_type=F32)


def mm_tn(a, b):
    return lax.dot_general(a, b, (((0,), (0,)), ((), ())), preferred_element_type=F32)


def sigmoid(x):
    return 0.5 * jnp.tanh(0.5 * x) + 0.5


def gather_kernel(req_ref, table_ref, out_ref):
    places = lax.broadcasted_iota(jnp.int32, (256, ROWS_DEV), 1)
    chosen = (places == req_ref[...]).astype(BF16)
    out_ref[...] = mm(chosen, table_ref[...]).astype(BF16)


def gather_rows(requested, table):
    count = requested.shape[0]
    return pl.pallas_call(
        gather_kernel,
        grid=(count // 256,),
        out_shape=jax.ShapeDtypeStruct((count, EMB), BF16),
        in_specs=[
            pl.BlockSpec((256, 1), lambda i: (i, 0)),
            pl.BlockSpec((ROWS_DEV, EMB), lambda i: (0, 0)),
        ],
        out_specs=pl.BlockSpec((256, EMB), lambda i: (i, 0)),
        compiler_params=pltpu.CompilerParams(vmem_limit_bytes=VMEM_LIMIT),
        name="gather_rows",
    )(requested, table)


def layer_kernel(
    rep_ref, cols_ref, rows_ref, up_ref, wp_ref, wo_ref, out_ref, g_ref,
    normed_t, mixed_t, tops, gbs,
):
    def pair(p, carry):
        start = pl.multiple_of(p * TOK, TOK)
        tokens = pl.ds(start, TOK)
        info = cols_ref[tokens, :]
        item_at, action_at = info[:, 0:1], info[:, 1:2]
        length = info[:, 2:3]
        replies = rep_ref[:, p].reshape(SLOTS, EMB)
        places = lax.broadcasted_iota(jnp.int32, (TOK, SLOTS), 1)
        left = mm((places == item_at).astype(BF16), replies)
        right = mm((places == action_at).astype(BF16), replies)
        fetched = jnp.concatenate([left, right], axis=1)
        average = jnp.mean(fetched, axis=1, keepdims=True)
        centred = fetched - average
        rstd = lax.rsqrt(jnp.mean(centred * centred, axis=1, keepdims=True) + EPSILON)
        normed_full = centred * rstd
        normed = normed_full.astype(BF16)
        normed_t[:, tokens] = normed_full.T.astype(BF16)

        before = mm(normed, wp_ref[...])
        gate = sigmoid(before)
        slope = gate * (1.0 + before * (1.0 - gate))
        projected = (before * gate).astype(BF16)
        u = projected[:, :D].astype(F32)
        values = projected[:, D : 2 * D]
        queries = projected[:, 2 * D : 2 * D + HEADS * QK]
        keys = projected[:, 2 * D + HEADS * QK :]

        at = lax.broadcasted_iota(jnp.int32, (TOK, TOK), 0)
        source = lax.broadcasted_iota(jnp.int32, (TOK, TOK), 1)
        seen = (source <= at) & ((at // SEQ) == (source // SEQ))
        share = jnp.where(seen, 1.0 / length.astype(F32), 0.0)
        lane = lax.broadcasted_iota(jnp.int32, (TOK, TOK), 1)
        parts = (lane < QK, lane >= QK)
        zero = jnp.zeros((TOK, TOK), BF16)

        weights, factors, attended = [], [], []
        for h in range(HEADS):
            two = slice((h // 2) * TOK, (h // 2 + 1) * TOK)
            key = jnp.where(parts[h % 2], keys[:, two], zero)
            score = mm_nt(queries[:, two], key)
            open_ = sigmoid(score)
            weight = (score * open_ * share).astype(BF16)
            weights.append(weight)
            factors.append(open_ * (1.0 + score * (1.0 - open_)) * share)
            attended.append(mm(weight, values[:, h * TOK : (h + 1) * TOK]))
        attended = jnp.concatenate(attended, axis=1)
        average = jnp.mean(attended, axis=1, keepdims=True)
        centred = attended - average
        spread = lax.rsqrt(jnp.mean(centred * centred, axis=1, keepdims=True) + EPSILON)
        inner = centred * spread
        mixed_t[:, tokens] = (inner * u).T.astype(BF16)

        place = lax.broadcasted_iota(jnp.int32, (TOK, D), 0) % SEQ
        top = jnp.where(place < length, up_ref[tokens, :].astype(F32), 0.0)
        top_low = top.astype(BF16)
        tops[tokens, :] = top_low
        grad_mixed = mm_nt(top_low, wo_ref[...]).astype(BF16).astype(F32)
        grad_u = (grad_mixed * inner).astype(BF16)
        grad_inner = grad_mixed * u
        first = jnp.mean(grad_inner, axis=1, keepdims=True)
        second = jnp.mean(grad_inner * inner, axis=1, keepdims=True)
        grad_att = (spread * (grad_inner - first - inner * second)).astype(BF16)

        grad_v, grad_q, grad_k = [], [], []
        for h in range(HEADS):
            own = slice(h * TOK, (h + 1) * TOK)
            two = slice((h // 2) * TOK, (h // 2 + 1) * TOK)
            grad_weight = mm_nt(grad_att[:, own], values[:, own]).astype(BF16).astype(F32)
            grad_v.append(mm_tn(weights[h], grad_att[:, own]).astype(BF16))
            grad_score = (grad_weight * factors[h]).astype(BF16)
            key = jnp.where(parts[h % 2], keys[:, two], zero)
            query = jnp.where(parts[h % 2], queries[:, two], zero)
            gq = mm(grad_score, key)
            gk = mm_tn(grad_score, query)
            if h % 2:
                grad_q[-1] = (grad_q[-1] + gq).astype(BF16)
                grad_k[-1] = (grad_k[-1] + gk).astype(BF16)
            else:
                grad_q.append(gq)
                grad_k.append(gk)
        grad_projected = jnp.concatenate([grad_u] + grad_v + grad_q + grad_k, axis=1)
        grad_before = (grad_projected.astype(F32) * slope).astype(BF16)
        gbs[tokens, :] = grad_before
        grad_normed = mm_nt(grad_before, wp_ref[...])
        first = jnp.mean(grad_normed, axis=1, keepdims=True)
        second = jnp.mean(grad_normed * normed_full, axis=1, keepdims=True)
        grad_rows = (top + rstd * (grad_normed - first - normed_full * second)).astype(BF16)

        slots = lax.broadcasted_iota(jnp.int32, (SLOTS, TOK), 0)
        item_row = rows_ref[p, 0:1, :]
        action_row = rows_ref[p, 1:2, :]
        back = mm((slots == item_row).astype(BF16), grad_rows[:, :EMB])
        back = back + mm((slots == action_row).astype(BF16), grad_rows[:, EMB:])
        out_ref[:, p] = back.astype(BF16).reshape(N_TABLE, 16, EMB)
        return carry

    lax.fori_loop(0, PAIRS, pair, 0)

    for y in range(N_DP // 2):
        wide = mm(normed_t[...], gbs[:, y * 768 : (y + 1) * 768]) * SCALE
        narrow = mm(mixed_t[...], tops[:, y * 256 : (y + 1) * 256]) * SCALE
        for c in range(2):
            g_ref[2 * y + c, :, 0:384] = wide[:, c * 384 : (c + 1) * 384].astype(BF16)
            g_ref[2 * y + c, :, 384:512] = narrow[:, c * 128 : (c + 1) * 128].astype(BF16)


def layer(replies, cols, rows, upstream, proj_weight, out_weight):
    whole = pl.BlockSpec(memory_space=pltpu.VMEM)
    return pl.pallas_call(
        layer_kernel,
        out_shape=(
            jax.ShapeDtypeStruct((N_TABLE, PAIRS, 16, EMB), BF16),
            jax.ShapeDtypeStruct((N_DP, D, 512), BF16),
        ),
        in_specs=[whole] * 6,
        out_specs=(whole, whole),
        scratch_shapes=[
            pltpu.VMEM((D, HIST * SEQ), BF16),
            pltpu.VMEM((D, HIST * SEQ), BF16),
            pltpu.VMEM((HIST * SEQ, D), BF16),
            pltpu.VMEM((HIST * SEQ, PROJ), BF16),
        ],
        compiler_params=pltpu.CompilerParams(vmem_limit_bytes=VMEM_LIMIT),
        name="layer",
    )(replies, cols, rows, upstream, proj_weight, out_weight)


class Ring:
    def __init__(self, place, to_right, to_left, chunk, half, far, near, send, recv):
        self.place, self.right, self.left = place, to_right, to_left
        self.chunk, self.half, self.far, self.near = chunk, half, far, near
        self.send, self.recv = send, recv

    def copy(self, number, src, dst, device):
        return pltpu.make_async_remote_copy(
            src_ref=src, dst_ref=dst, send_sem=self.send.at[number], recv_sem=self.recv.at[number],
            device_id=device, device_id_type=MESH,
        )

    def begin(self):
        across, after, ahead = (lax.rem(self.place + k, 4) for k in (2, 1, 3))
        self.after, self.ahead = after, ahead
        part, half, far, near = self.chunk, self.half, self.far, self.near
        self.copies = [
            self.copy(0, half(part(across), 0), far.at[0], self.right),
            self.copy(1, half(part(across), 1), far.at[1], self.left),
            self.copy(2, half(part(after), 1), half(near.at[0], 1), self.right),
            self.copy(3, half(part(ahead), 0), half(near.at[1], 0), self.left),
            self.copy(4, half(part(after), 0), half(near.at[0], 0), self.right),
            self.copy(5, half(part(ahead), 1), half(near.at[1], 1), self.left),
        ]
        for k in range(4):
            self.copies[k].start()

    def forward(self, add):
        self.copies[0].wait_recv()
        add(self.half(self.chunk(self.after), 0), self.far.at[0])
        self.copies[4].start()
        self.copies[1].wait_recv()
        add(self.half(self.chunk(self.ahead), 1), self.far.at[1])
        self.copies[5].start()

    def arrive(self):
        for k in range(2, 6):
            self.copies[k].wait_recv()

    def end(self):
        for k in range(6):
            self.copies[k].wait_send()


def add_into(target, other):
    for n in range(target.shape[0]):
        target[n] = (target[n].astype(F32) + other[n].astype(F32)).astype(BF16)


def finish_kernel(
    g_ref, slots_ref, req_ref, dense_ref, table_ref,
    core_buf, s1, far_a, far_b, near_a, near_b, sum_a, sum_b,
    far_a2, far_b2, near_a2, near_b2, s4, zbuf, incoming, t2, t_core, t_far, t_near,
    core_send, core_recv, ring_send, ring_recv, z_send, z_recv, a_send, a_recv, own_sem,
):
    dp = lax.axis_index("dp")
    tab = lax.axis_index("table")
    y, c = dp // 2, dp % 2
    x, z = tab // 8, tab % 8
    other = (2 * y + 1 - c, tab)
    y_right = (2 * lax.rem(y + 1, 4) + c, tab)
    y_left = (2 * lax.rem(y + 3, 4) + c, tab)
    x_right = (dp, lax.rem(tab + 8, 32))
    x_left = (dp, lax.rem(tab + 24, 32))

    barrier = pltpu.get_barrier_semaphore()
    for device in (other, y_right, y_left):
        pl.semaphore_signal(barrier, inc=1, device_id=device, device_id_type=MESH)

    def greet(k, carry):
        pl.semaphore_signal(
            barrier, inc=1, device_id=(dp, lax.rem(tab + k, 32)), device_id_type=MESH
        )
        return carry

    lax.fori_loop(1, 32, greet, 0)
    pl.semaphore_wait(barrier, 34)

    def core_copy(k):
        return pltpu.make_async_remote_copy(
            src_ref=g_ref.at[2 * k + 1 - c], dst_ref=core_buf.at[k],
            send_sem=core_send.at[k], recv_sem=core_recv.at[k],
            device_id=other, device_id_type=MESH,
        )

    for k in range(4):
        core_copy(k).start()

    def give_copy(k):
        peer = lax.rem(tab + k, 32)
        return pltpu.make_async_remote_copy(
            src_ref=slots_ref.at[peer], dst_ref=incoming.at[tab],
            send_sem=a_send.at[k], recv_sem=a_recv.at[k],
            device_id=(dp, peer), device_id_type=MESH,
        )

    def give(k, carry):
        give_copy(k).start()
        return carry

    lax.fori_loop(1, 32, give, 0)
    own = pltpu.make_async_copy(slots_ref.at[tab], incoming.at[tab], own_sem)
    own.start()

    def merge(k):
        def step(n, carry):
            rows = pl.ds(pl.multiple_of(n * 256, 256), 256)
            mine = g_ref[2 * k + c, rows, :].astype(F32)
            s1[k, n] = (mine + core_buf[k, rows, :].astype(F32)).astype(BF16)
            return carry

        lax.fori_loop(0, 4, step, 0)

    for k in range(4):
        core_copy(k).wait_recv()
        merge(k)

    def two(ref, n):
        return ref.at[pl.ds(2 * n, 2)]

    ring_a = Ring(y, y_right, y_left, lambda k: s1.at[k, :, pl.ds(0, 128), :], two, far_a, near_a,
                  ring_send.at[0], ring_recv.at[0])
    ring_b = Ring(x, x_right, x_left, lambda k: s1.at[:, k, pl.ds(128, 128), :], two, far_b, near_b,
                  ring_send.at[1], ring_recv.at[1])
    ring_a.begin()
    ring_b.begin()
    ring_a.forward(add_into)
    ring_b.forward(add_into)
    ring_a.arrive()
    for n in range(4):
        sum_a[n] = (
            s1[y, n, 0:128, :].astype(F32) + near_a[0, n].astype(F32) + near_a[1, n].astype(F32)
        ).astype(BF16)

    def rows64(ref, n):
        return ref.at[pl.ds(64 * n, 64), :]

    def add_flat(target, other_ref):
        target[...] = (target[...].astype(F32) + other_ref[...].astype(F32)).astype(BF16)

    ring_a2 = Ring(x, x_right, x_left, lambda k: sum_a.at[k], rows64, far_a2, near_a2,
                   ring_send.at[2], ring_recv.at[2])
    ring_a2.begin()
    ring_b.arrive()
    for n in range(4):
        sum_b[n] = (
            s1[n, x, 128:256, :].astype(F32) + near_b[0, n].astype(F32) + near_b[1, n].astype(F32)
        ).astype(BF16)
    ring_b2 = Ring(y, y_right, y_left, lambda k: sum_b.at[k], rows64, far_b2, near_b2,
                   ring_send.at[3], ring_recv.at[3])
    ring_b2.begin()
    ring_a2.forward(add_flat)
    ring_b2.forward(add_flat)
    ring_a2.arrive()
    low = sum_a[x].astype(F32) + near_a2[0].astype(F32) + near_a2[1].astype(F32)
    s4[0:4] = low.astype(BF16).reshape(4, 32, 512)
    ring_b2.arrive()
    high = sum_b[y].astype(F32) + near_b2[0].astype(F32) + near_b2[1].astype(F32)
    s4[4:8] = high.astype(BF16).reshape(4, 32, 512)

    def z_copy(k):
        peer = lax.rem(z + k, 8)
        return pltpu.make_async_remote_copy(
            src_ref=s4.at[peer], dst_ref=zbuf.at[k],
            send_sem=z_send.at[k], recv_sem=z_recv.at[k],
            device_id=(dp, 8 * x + peer), device_id_type=MESH,
        )

    for k in range(1, 8):
        z_copy(k).start()

    def taken(k, carry):
        give_copy(k).wait_recv()
        return carry

    own.wait()
    lax.fori_loop(1, 32, taken, 0)

    def rows_of(first):
        places = lax.broadcasted_iota(jnp.int32, (256, ROWS_DEV), 0) + first
        chosen = (places == req_ref[...]).astype(BF16)
        return mm(chosen, incoming[...].reshape(N_TABLE * 64, EMB)).astype(BF16).astype(F32)

    def table_block(b, carry):
        upper = rows_of(b * 256)
        lower = rows_of(b * 256 + 1024)
        rows = pl.ds(pl.multiple_of(b * 256, 256), 256)
        is_left = lax.broadcasted_iota(jnp.int32, (256, 128), 1) < 64
        for k in range(4):
            up, low = upper[:, k * 128 : (k + 1) * 128], lower[:, k * 128 : (k + 1) * 128]
            t2[0, k, rows, :] = jnp.where(is_left, up, pltpu.roll(low, 64, 1)).astype(BF16)
            t2[1, k, rows, :] = jnp.where(is_left, pltpu.roll(up, 64, 1), low).astype(BF16)
        return carry

    lax.fori_loop(0, 4, table_block, 0)
    t_copy = pltpu.make_async_remote_copy(
        src_ref=t2.at[1 - c], dst_ref=t_core, send_sem=core_send.at[4], recv_sem=core_recv.at[4],
        device_id=other, device_id_type=MESH,
    )
    t_copy.start()

    total = s4[z].astype(F32)
    for k in range(1, 8):
        z_copy(k).wait_recv()
        total = total + zbuf[k].astype(F32)
    dense_ref[...] = total.astype(BF16)

    t_copy.wait_recv()
    for k in range(4):
        add_flat(t2.at[c, k], t_core.at[k])

    def rows512(ref, n):
        return ref.at[pl.ds(512 * n, 512), :]

    ring_t = Ring(y, y_right, y_left, lambda k: t2.at[c, k], rows512, t_far, t_near,
                  ring_send.at[4], ring_recv.at[4])
    ring_t.begin()
    ring_t.forward(add_flat)
    ring_t.arrive()
    table_ref[...] = (
        t2[c, y].astype(F32) + t_near[0].astype(F32) + t_near[1].astype(F32)
    ).astype(BF16)

    def sent(k, carry):
        give_copy(k).wait_send()
        return carry

    lax.fori_loop(1, 32, sent, 0)
    for k in range(4):
        core_copy(k).wait_send()
    for k in range(1, 8):
        z_copy(k).wait_send()
    t_copy.wait_send()
    for ring in (ring_a, ring_b, ring_a2, ring_b2, ring_t):
        ring.end()


def finish(dense_terms, outgoing, requested):
    whole = pl.BlockSpec(memory_space=pltpu.VMEM)
    dma = pltpu.SemaphoreType.DMA
    return pl.pallas_call(
        finish_kernel,
        out_shape=(
            jax.ShapeDtypeStruct((32, 512), BF16),
            jax.ShapeDtypeStruct((1024, 128), BF16),
        ),
        in_specs=[whole] * 3,
        out_specs=(whole, whole),
        scratch_shapes=[
            pltpu.VMEM((4, D, 512), BF16),
            pltpu.VMEM((4, 4, 256, 512), BF16),
            pltpu.VMEM((2, 2, 128, 512), BF16),
            pltpu.VMEM((2, 2, 128, 512), BF16),
            pltpu.VMEM((2, 4, 128, 512), BF16),
            pltpu.VMEM((2, 4, 128, 512), BF16),
            pltpu.VMEM((4, 128, 512), BF16),
            pltpu.VMEM((4, 128, 512), BF16),
            pltpu.VMEM((2, 64, 512), BF16),
            pltpu.VMEM((2, 64, 512), BF16),
            pltpu.VMEM((2, 128, 512), BF16),
            pltpu.VMEM((2, 128, 512), BF16),
            pltpu.VMEM((8, 32, 512), BF16),
            pltpu.VMEM((8, 32, 512), BF16),
            pltpu.VMEM((N_TABLE, 64, EMB), BF16),
            pltpu.VMEM((2, 4, 1024, 128), BF16),
            pltpu.VMEM((4, 1024, 128), BF16),
            pltpu.VMEM((2, 512, 128), BF16),
            pltpu.VMEM((2, 1024, 128), BF16),
            dma((5,)), dma((5,)), dma((5, 6)), dma((5, 6)), dma((8,)), dma((8,)),
            dma((32,)), dma((32,)), dma,
        ],
        compiler_params=pltpu.CompilerParams(
            vmem_limit_bytes=VMEM_LIMIT, collective_id=0, has_side_effects=True
        ),
        name="finish",
    )(dense_terms, outgoing, requested)


def body(
    embed_table, owner_shard, slot_row, lengths, send_order, proj_weight, out_weight, upstream
):
    order = send_order[0]
    ids = owner_shard[..., 0] * ROWS_DEV + slot_row
    ids = jnp.swapaxes(ids, 1, 2).reshape(HIST, 2 * SEQ)
    message = jnp.concatenate([ids, lengths[:, None]], axis=1)[order]
    message = lax.all_to_all(message, "dp", split_axis=0, concat_axis=0, tiled=True)
    ids, length = message[:, : 2 * SEQ], message[:, 2 * SEQ]
    owner, row = ids // ROWS_DEV, ids % ROWS_DEV
    same = owner[:, :, None] == owner[:, None, :]
    earlier = jnp.tril(jnp.ones((2 * SEQ, 2 * SEQ), jnp.bool_), -1)
    rank = jnp.sum((same & earlier[None]).astype(jnp.int32), axis=2)
    slot = owner * MOST + rank
    hit = slot[:, None, :] == jnp.arange(N_TABLE * MOST)[None, :, None]
    request = jnp.sum(jnp.where(hit, row[:, None, :] + 1, 0), axis=2) - 1
    request = request.reshape(HIST, N_TABLE, MOST).transpose(1, 0, 2).reshape(N_TABLE, 64)
    requested = lax.all_to_all(request, "table", split_axis=0, concat_axis=0, tiled=True)

    picked = gather_rows(requested.reshape(-1, 1), embed_table).reshape(N_TABLE, 64, EMB)
    replies = lax.all_to_all(picked, "table", split_axis=0, concat_axis=0, tiled=True)

    in_pair = owner * 16 + (jnp.arange(HIST) % 2)[:, None] * MOST + rank
    in_pair = in_pair.reshape(PAIRS, 2, 2, SEQ)
    rows = jnp.swapaxes(in_pair, 1, 2).reshape(PAIRS, 2, TOK)
    cols = jnp.stack(
        [
            in_pair[:, :, 0].reshape(-1),
            in_pair[:, :, 1].reshape(-1),
            jnp.broadcast_to(length[:, None], (HIST, SEQ)).reshape(-1),
        ],
        axis=1,
    )
    outgoing, dense_terms = layer(
        replies.reshape(N_TABLE, PAIRS, 16, EMB),
        cols,
        rows,
        upstream.reshape(HIST * SEQ, D),
        proj_weight,
        out_weight,
    )
    dense, table = finish(
        dense_terms, outgoing.reshape(N_TABLE, 64, EMB), requested.reshape(1, -1)
    )
    table = jnp.concatenate([table[:, :64], table[:, 64:]], axis=0)
    return table, dense[:, :384], dense[:, 384:]


def solution(mesh):
    in_specs = (
        P("table", None),
        P(("dp", "table"), None, None, None),
        P(("dp", "table"), None, None),
        P(("dp", "table")),
        P(("dp", "table"), None),
        P(),
        P(),
        P(("dp", "table"), None, None),
    )
    out_specs = (P("table", "dp"), P("table", "dp"), P("table", "dp"))
    return jax.shard_map(body, mesh=mesh, in_specs=in_specs, out_specs=out_specs, check_vma=False)
```

time: 550 us -> 233 us (0.42); the launches traced: 541 us -> 232 us
  waiting for transfers between devices: 304 us -> 50.9 us
  Pallas kernels: 0 us -> 134 us
  local copies, waits for them, and re-layouts: 77 us -> 13.5 us
  other arithmetic: 55.2 us -> 3.2 us
  matrix products: 30.5 us -> 0 us
  blocking collectives: 38.8 us -> 19 us
  between operations: 14.4 us -> 0.73 us
  starting transfers between devices: 21 us -> 10.7 us
    reduce_scatter x2 -> x0, waiting for transfers between devices: 209 us -> none  [the longest x1 201 us: body(): lax.psum_scatter(jnp.concatenate([first, second], axis=2).reshape(count,...]
    pallas_call x0 -> x3, Pallas kernels: none -> 134 us  [the longest x1 84.1 us: finish(): pl.pallas_call(finish_kernel, out_shape=(jax.ShapeDtypeStruct((32, 512),...]
    unnamed x4 -> x0, waiting for transfers between devices: 35.2 us -> none
    dot_general x11 -> x0, matrix products: 30.5 us -> none  [the longest x1 8.66 us: local_layer(): before = jnp.dot(normed, proj_weight, preferred_element_type=jnp.float32)]
    unnamed x39 -> x4, local copies, waits for them, and re-layouts: 25.4 us -> 2.2 us
    all_to_all x2 -> x1, blocking collectives: 38.8 us -> 19 us  [body(): lax.all_to_all(request, 'table', split_axis=0, concat_axis=0, tiled=True)]
    scatter-add x1 -> x0, other arithmetic: 16.6 us -> none  [give_back(): jnp.zeros((row_count, emb_width), jnp.float32)]
    gather x8 -> x1, local copies, waits for them, and re-layouts: 16.7 us -> 0.56 us  [body(): message = jnp.concatenate([ids, lengths[:, None]], axis=1)[order]]
  transfers between devices with their start and end apart: 7 -> 2, of which waited for: 5 -> 2; matrix products, arithmetic and copies ran while one was open for 10% -> 1% of each run, Pallas kernels for 0% -> 0%
where the time goes in v1:
time: 233 us; the launch traced here: 232 us
  Pallas kernels  134 us (58%)
  waiting for transfers between devices  50.9 us (22%)
  blocking collectives  19 us (8%)
  local copies, waits for them, and re-layouts  13.5 us (6%)
  starting transfers between devices  10.7 us (5%)
  other arithmetic  3.2 us (1%)
    pallas_call x1, Pallas kernels, finish(): pl.pallas_call(finish_kernel, out_shape=(jax.ShapeDtypeStruct((32, 512),...  84.1 us
    all_to_all x1, waiting for transfers between devices, body(): lax.all_to_all(picked, 'table', split_axis=0, concat_axis=0, tiled=True)  46.4 us
    pallas_call x1, Pallas kernels, layer(): pl.pallas_call(layer_kernel, out_shape=(jax.ShapeDtypeStruct((N_TABLE, PA...  41.1 us
    all_to_all x1, blocking collectives, body(): lax.all_to_all(request, 'table', split_axis=0, concat_axis=0, tiled=True)  19 us
    pallas_call x1, Pallas kernels, gather_rows(): pl.pallas_call(gather_kernel, grid=(count // 256,), out_shape=jax.ShapeDt...  9.19 us
    all_to_all x1, starting transfers between devices, body(): lax.all_to_all(message, 'dp', split_axis=0, concat_axis=0, tiled=True)  6.48 us
  transfers between devices with their start and end apart: 2, of which 2 were waited for; matrix products, arithmetic and copies ran while one was open for 1% of the time, Pallas kernels for 0%

profile of v1, /device:TPU:1, one launch (start us, length us, event | category | flops | bytes accessed | tf_op | source)
XLA Modules:
  0.0 232.4 jit_solution(14091748115089784411)
XLA Ops:
  0.6 0.7 fusion.5
  1.3 0.7 copy.42
  2.0 0.7 fusion
  2.8 0.6 gather_fusion
  3.4 0.6 copy.43
  4.0 6.5 %all-to-all-start = ((s32[8,1,129]{2,1,0:T(1,128)}), s32[8,1,129]{2,1,0:T(1,128)S(1)}, u32[]{:S(2)}, u32[]{:S(2)}) async-start(s32[8,1,129]{2,1,0:T(1,128)} %copy.43), calls=%async_computation | async-start | bytes 16384 | tf_op jit(solution)/shard_map/all_to_all | solution.py:486
  10.5 0.1 iota_compare_fusion.1
  10.6 4.5 %all-to-all-done = s32[8,1,129]{2,1,0:T(1,128)S(1)} async-done(((s32[8,1,129]{2,1,0:T(1,128)}), s32[8,1,129]{2,1,0:T(1,128)S(1)}, u32[]{:S(2)}, u32[]{:S(2)}) %all-to-all-start) | async-done | bytes 4160 | tf_op jit(solution)/shard_map/all_to_all | solution.py:486
  15.1 0.4 convert_reduce_fusion
  15.6 0.4 select_reduce_fusion
  16.0 0.1 sub.14
  16.2 0.1 copy.44
  16.3 19.0 %all_to_all.26 = s32[32,1,64]{2,1,0:T(1,128)S(1)} all-to-all(s32[32,1,64]{2,1,0:T(1,128)S(1)} %copy.45), channel_id=1, replica_groups=mesh['dp'=8,'table'=32] {'table'}, dimensions={0} | all-to-all | bytes 16384 | tf_op jit(solution)/shard_map/all_to_all | solution.py:496
  35.3 0.5 broadcast.116
  35.8 0.7 reduce.7
  36.5 2.0 reshape.121.req_ref
  38.5 9.2 %gather_rows.1 = bf16[2048,512]{1,0:T(8,128)(2,1)} custom-call(s32[2048,1]{1,0:T(8,128)} %reshape.121.req_ref, bf16[2048,512]{1,0:T(8,128)(2,1)} %table_ref.1), custom_call_target="tpu_custom_call" | custom-call | tf_op jit(solution)/shard_map/gather_rows/pallas_call | solution.py:56
  47.7 4.2 %all-to-all-start.2 = ((bf16[32,64,512]{2,1,0:T(8,128)(2,1)}), bf16[32,64,512]{2,1,0:T(8,128)(2,1)S(1)}, u32[]{:S(2)}, u32[]{:S(2)}) async-start(bf16[32,64,512]{2,1,0:T(8,128)(2,1)} %bitcast.32), calls=%async_computation.2 | async-start | bytes 4194304 | tf_op jit(solution)/shard_map/all_to_all | solution.py:499
  51.9 0.1 slice_reduce_fusion
  52.2 0.7 reshape.109.rows_ref
  52.9 0.1 stack_reshape_squeeze.6
  53.1 0.9 copy.50.cols_ref
  53.9 0.7 reshape.112.req_ref
  54.6 46.4 %all-to-all-done.2 = bf16[32,64,512]{2,1,0:T(8,128)(2,1)S(1)} async-done(((bf16[32,64,512]{2,1,0:T(8,128)(2,1)}), bf16[32,64,512]{2,1,0:T(8,128)(2,1)S(1)}, u32[]{:S(2)}, u32[]{:S(2)}) %all-to-all-start.2) | async-done | bytes 2097184 | tf_op jit(solution)/shard_map/all_to_all | solution.py:499
  101.0 1.3 copy-done
  102.3 41.1 %layer.1 = (bf16[32,4,16,512]{3,2,1,0:T(8,128)(2,1)}, bf16[8,1024,512]{2,1,0:T(8,128)(2,1)}) custom-call(bf16[32,4,16,512]{3,2,1,0:T(8,128)(2,1)} %bitcast.33, s32[512,3]{1,0:T(8,128)} %copy.50.cols_ref, s32[4,2,128]{2,1,0:T(2,128)} %reshape.109.rows_ref, bf16[512,1024]{1,0:T(8,128)(2,1)} %bitcast.35, bf16[1024,3072]{1,0:T(8,128)(2,1)} %wp_ref.1, ...), custom_call_target="tpu_custom_call" | custom-call | tf_op jit(solution)/shard_map/layer/pallas_call | solution.py:182
  143.4 84.1 %finish.1 = (bf16[32,512]{1,0:T(8,128)(2,1)}, bf16[1024,128]{1,0:T(8,128)(2,1)}) custom-call(bf16[8,1024,512]{2,1,0:T(8,128)(2,1)} %get-tuple-element.7.g_ref, bf16[32,64,512]{2,1,0:T(8,128)(2,1)} %bitcast.34, s32[1,2048]{1,0:T(1,128)} %reshape.112.req_ref), custom_call_target="tpu_custom_call" | custom-call | tf_op jit(solution)/shard_map/finish/pallas_call | solution.py:441
  227.5 1.3 slice.31
  228.8 1.3 slice.30
  230.2 1.2 fusion.6
  231.3 0.1 pad_maximum_fusion
  231.5 0.9 copy.51
  (18 shorter events, 0.6 us)
Async XLA Ops:
  4.0 11.1 %all-to-all-start = ((s32[8,1,129]{2,1,0:T(1,128)}), s32[8,1,129]{2,1,0:T(1,128)S(1)}, u32[]{:S(2)}, u32[]{:S(2)}) async-start(s32[8,1,129]{2,1,0:T(1,128)} %copy.43), calls=%async_computation | async-start | bytes 16384 | tf_op jit(solution)/shard_map/all_to_all | solution.py:486
  47.7 53.4 %all-to-all-start.2 = ((bf16[32,64,512]{2,1,0:T(8,128)(2,1)}), bf16[32,64,512]{2,1,0:T(8,128)(2,1)S(1)}, u32[]{:S(2)}, u32[]{:S(2)}) async-start(bf16[32,64,512]{2,1,0:T(8,128)(2,1)} %bitcast.32), calls=%async_computation.2 | async-start | bytes 4194304 | tf_op jit(solution)/shard_map/all_to_all | solution.py:499
  101.0 1.3 copy-start

commit v2 on v1

v2 whole, which is shorter than its diff:
```python
import functools

import jax
import jax.numpy as jnp
from jax import lax
from jax.experimental import pallas as pl
from jax.experimental.pallas import tpu as pltpu
from jax.sharding import PartitionSpec as P

D = 1024
EMB = 512
HEADS = 8
QK = 64
PROJ = 3072
SEQ = 64
HIST = 8
ROWS_DEV = 2048
MOST = 8
N_DP = 8
N_TABLE = 32
PAIRS = HIST // 2
TOK = 2 * SEQ
SLOTS = 2 * N_TABLE * MOST
EPSILON = 1e-06
SCALE = float(2048 * 64) ** (-0.5)
MESH = pl.DeviceIdType.MESH
VMEM_LIMIT = 60 * 1024 * 1024
F32 = jnp.float32
BF16 = jnp.bfloat16


def mm(a, b):
    return lax.dot_general(a, b, (((1,), (0,)), ((), ())), preferred_element_type=F32)


def mm_nt(a, b):
    return lax.dot_general(a, b, (((1,), (1,)), ((), ())), preferred_element_type=F32)


def mm_tn(a, b):
    return lax.dot_general(a, b, (((0,), (0,)), ((), ())), preferred_element_type=F32)


def sigmoid(x):
    return 0.5 * jnp.tanh(0.5 * x) + 0.5


class Ring:
    def __init__(self, place, to_right, to_left, chunk, half, far, near, send, recv):
        self.place, self.right, self.left = place, to_right, to_left
        self.chunk, self.half, self.far, self.near = chunk, half, far, near
        self.send, self.recv = send, recv

    def copy(self, number, src, dst, device):
        return pltpu.make_async_remote_copy(
            src_ref=src, dst_ref=dst, send_sem=self.send.at[number], recv_sem=self.recv.at[number],
            device_id=device, device_id_type=MESH,
        )

    def begin(self):
        across, after, ahead = (lax.rem(self.place + k, 4) for k in (2, 1, 3))
        self.after, self.ahead = after, ahead
        part, half, far, near = self.chunk, self.half, self.far, self.near
        self.copies = [
            self.copy(0, half(part(across), 0), far.at[0], self.right),
            self.copy(1, half(part(across), 1), far.at[1], self.left),
            self.copy(2, half(part(after), 1), half(near.at[0], 1), self.right),
            self.copy(3, half(part(ahead), 0), half(near.at[1], 0), self.left),
            self.copy(4, half(part(after), 0), half(near.at[0], 0), self.right),
            self.copy(5, half(part(ahead), 1), half(near.at[1], 1), self.left),
        ]
        for k in range(4):
            self.copies[k].start()

    def forward(self, add):
        self.copies[0].wait_recv()
        add(self.half(self.chunk(self.after), 0), self.far.at[0])
        self.copies[4].start()
        self.copies[1].wait_recv()
        add(self.half(self.chunk(self.ahead), 1), self.far.at[1])
        self.copies[5].start()

    def arrive(self):
        for k in range(2, 6):
            self.copies[k].wait_recv()

    def end(self):
        for k in range(6):
            self.copies[k].wait_send()


def add_into(target, other):
    for n in range(target.shape[0]):
        target[n] = (target[n].astype(F32) + other[n].astype(F32)).astype(BF16)


def layer_pair(replies, cols, rows, upstream, wp, wo):
    item_at, action_at, length = cols[:, 0:1], cols[:, 1:2], cols[:, 2:3]
    places = lax.broadcasted_iota(jnp.int32, (TOK, SLOTS), 1)
    left = mm((places == item_at).astype(BF16), replies)
    right = mm((places == action_at).astype(BF16), replies)
    fetched = jnp.concatenate([left, right], axis=1)
    average = jnp.mean(fetched, axis=1, keepdims=True)
    centred = fetched - average
    rstd = lax.rsqrt(jnp.mean(centred * centred, axis=1, keepdims=True) + EPSILON)
    normed_full = centred * rstd
    normed = normed_full.astype(BF16)

    before = mm(normed, wp[...])
    gate = sigmoid(before)
    slope = gate * (1.0 + before * (1.0 - gate))
    projected = (before * gate).astype(BF16)
    u = projected[:, :D].astype(F32)
    values = projected[:, D : 2 * D]
    queries = projected[:, 2 * D : 2 * D + HEADS * QK]
    keys = projected[:, 2 * D + HEADS * QK :]

    at = lax.broadcasted_iota(jnp.int32, (TOK, TOK), 0)
    source = lax.broadcasted_iota(jnp.int32, (TOK, TOK), 1)
    seen = (source <= at) & ((at // SEQ) == (source // SEQ))
    share = jnp.where(seen, 1.0 / length.astype(F32), 0.0)
    parts = (source < QK, source >= QK)
    zero = jnp.zeros((TOK, TOK), BF16)

    weights, factors, attended = [], [], []
    for h in range(HEADS):
        two = slice((h // 2) * TOK, (h // 2 + 1) * TOK)
        key = jnp.where(parts[h % 2], keys[:, two], zero)
        score = mm_nt(queries[:, two], key)
        open_ = sigmoid(score)
        weight = (score * open_ * share).astype(BF16)
        weights.append(weight)
        factors.append(open_ * (1.0 + score * (1.0 - open_)) * share)
        attended.append(mm(weight, values[:, h * TOK : (h + 1) * TOK]))
    attended = jnp.concatenate(attended, axis=1)
    average = jnp.mean(attended, axis=1, keepdims=True)
    centred = attended - average
    spread = lax.rsqrt(jnp.mean(centred * centred, axis=1, keepdims=True) + EPSILON)
    inner = centred * spread
    mixed = inner * u

    place = lax.broadcasted_iota(jnp.int32, (TOK, D), 0) % SEQ
    top = jnp.where(place < length, upstream.astype(F32), 0.0)
    top_low = top.astype(BF16)
    grad_mixed = mm_nt(top_low, wo[...]).astype(BF16).astype(F32)
    grad_u = (grad_mixed * inner).astype(BF16)
    grad_inner = grad_mixed * u
    first = jnp.mean(grad_inner, axis=1, keepdims=True)
    second = jnp.mean(grad_inner * inner, axis=1, keepdims=True)
    grad_att = (spread * (grad_inner - first - inner * second)).astype(BF16)

    grad_v, grad_q, grad_k = [], [], []
    for h in range(HEADS):
        own = slice(h * TOK, (h + 1) * TOK)
        two = slice((h // 2) * TOK, (h // 2 + 1) * TOK)
        grad_weight = mm_nt(grad_att[:, own], values[:, own]).astype(BF16).astype(F32)
        grad_v.append(mm_tn(weights[h], grad_att[:, own]).astype(BF16))
        grad_score = (grad_weight * factors[h]).astype(BF16)
        key = jnp.where(parts[h % 2], keys[:, two], zero)
        query = jnp.where(parts[h % 2], queries[:, two], zero)
        gq = mm(grad_score, key)
        gk = mm_tn(grad_score, query)
        if h % 2:
            grad_q[-1] = (grad_q[-1] + gq).astype(BF16)
            grad_k[-1] = (grad_k[-1] + gk).astype(BF16)
        else:
            grad_q.append(gq)
            grad_k.append(gk)
    grad_projected = jnp.concatenate([grad_u] + grad_v + grad_q + grad_k, axis=1)
    grad_before = (grad_projected.astype(F32) * slope).astype(BF16)
    grad_normed = mm_nt(grad_before, wp[...])
    first = jnp.mean(grad_normed, axis=1, keepdims=True)
    second = jnp.mean(grad_normed * normed_full, axis=1, keepdims=True)
    grad_rows = (top + rstd * (grad_normed - first - normed_full * second)).astype(BF16)

    slots = lax.broadcasted_iota(jnp.int32, (SLOTS, TOK), 0)
    back = mm((slots == rows[0:1, :]).astype(BF16), grad_rows[:, :EMB])
    back = back + mm((slots == rows[1:2, :]).astype(BF16), grad_rows[:, EMB:])
    return normed_full.T.astype(BF16), mixed.T.astype(BF16), top_low, grad_before, back.astype(BF16)


def split_number(numbers):
    high = numbers // 256
    return (numbers - 256 * high).astype(BF16), high.astype(BF16)


def program_kernel(
    msg_ref, order_ref, table_hbm, up_hbm, wp_hbm, wo_hbm,
    proj_ref, outw_ref, table_ref,
    table, up, wp, wo, msg_out, msg_in, req_out, req_in, wanted, req_rows, rows_s, cols_s,
    picked, replies, outgoing, incoming, normed_t, mixed_t, tops, gbs,
    g, core_buf, far_a, far_b, near_a, near_b, sum_a, sum_b,
    far_a2, far_b2, near_a2, near_b2, s4, zbuf, t2, t_core, t_far, t_near,
    load_sem, m_send, m_recv, r_send, r_recv, f_send, f_recv, a_send, a_recv,
    core_send, core_recv, ring_send, ring_recv, z_send, z_recv,
):
    dp = lax.axis_index("dp")
    tab = lax.axis_index("table")
    y, c = dp // 2, dp % 2
    x, z = tab // 8, tab % 8
    other = (2 * y + 1 - c, tab)
    y_right = (2 * lax.rem(y + 1, 4) + c, tab)
    y_left = (2 * lax.rem(y + 3, 4) + c, tab)
    x_right = (dp, lax.rem(tab + 8, 32))
    x_left = (dp, lax.rem(tab + 24, 32))

    loads = [
        pltpu.make_async_copy(src, dst, load_sem.at[n])
        for n, (src, dst) in enumerate(
            ((table_hbm, table), (up_hbm, up), (wp_hbm, wp), (wo_hbm, wo))
        )
    ]
    for load in loads:
        load.start()

    barrier = pltpu.get_barrier_semaphore()

    def greet_dp(k, carry):
        pl.semaphore_signal(
            barrier, inc=1, device_id=(lax.rem(dp + k, 8), tab), device_id_type=MESH
        )
        return carry

    def greet_table(k, carry):
        pl.semaphore_signal(
            barrier, inc=1, device_id=(dp, lax.rem(tab + k, 32)), device_id_type=MESH
        )
        return carry

    lax.fori_loop(1, 8, greet_dp, 0)
    lax.fori_loop(1, 32, greet_table, 0)

    order = order_ref[...]
    message = jnp.zeros((HIST, 256), jnp.int32)
    for m in range(HIST):
        message = message + jnp.where(order == m, msg_ref[m : m + 1, :], 0)
    for k in range(HIST):
        msg_out[k] = message[k : k + 1, :]
    pl.semaphore_wait(barrier, 38)

    def msg_copy(k):
        peer = lax.rem(dp + k, 8)
        return pltpu.make_async_remote_copy(
            src_ref=msg_out.at[peer], dst_ref=msg_in.at[dp],
            send_sem=m_send.at[k], recv_sem=m_recv.at[k],
            device_id=(peer, tab), device_id_type=MESH,
        )

    for k in range(1, 8):
        msg_copy(k).start()
    msg_in[dp] = msg_out[dp]
    for k in range(1, 8):
        msg_copy(k).wait_recv()

    got = jnp.concatenate([msg_in[k] for k in range(HIST)], axis=0)
    ids, lengths = got[:, : 2 * SEQ], got[:, 2 * SEQ : 2 * SEQ + 1]
    owner = ids // ROWS_DEV
    ids_col = ids.astype(F32).T.astype(jnp.int32)
    owner_col, row_col = ids_col // ROWS_DEV, ids_col % ROWS_DEV
    sub = lax.broadcasted_iota(jnp.int32, (TOK, TOK), 0)
    lane = lax.broadcasted_iota(jnp.int32, (TOK, TOK), 1)
    ranks = []
    for m in range(HIST):
        same = (owner_col[:, m : m + 1] == owner[m : m + 1, :]) & (sub < lane)
        ranks.append(jnp.sum(jnp.where(same, 1.0, 0.0), axis=0, keepdims=True))
    rank = jnp.concatenate(ranks, axis=0)
    rank_col = rank.T.astype(jnp.int32)
    request = jnp.zeros((N_TABLE, TOK), F32)
    owners = lax.broadcasted_iota(jnp.int32, (N_TABLE, TOK), 0)
    for m in range(HIST):
        low, high = split_number(row_col[:, m : m + 1] + 1)
        spot = m * MOST + rank_col[:, m : m + 1]
        put = jnp.where(lane == spot, low.astype(F32), 0.0)
        put = jnp.where(lane == spot + 64, high.astype(F32), put)
        request = request + mm((owners == owner[m : m + 1, :]).astype(BF16), put.astype(BF16))
    request = request + 256.0 * pltpu.roll(request, 64, 1)
    request = jnp.where(owners >= 0, request, 0.0)
    request = jnp.where(lax.broadcasted_iota(jnp.int32, (N_TABLE, TOK), 1) < 64, request, 0.0)
    request = request.astype(jnp.int32)
    for o in range(N_TABLE):
        req_out[o] = request[o : o + 1, :]

    def req_copy(k):
        peer = lax.rem(tab + k, 32)
        return pltpu.make_async_remote_copy(
            src_ref=req_out.at[peer], dst_ref=req_in.at[tab],
            send_sem=r_send.at[k], recv_sem=r_recv.at[k],
            device_id=(dp, peer), device_id_type=MESH,
        )

    def ask(k, carry):
        req_copy(k).start()
        return carry

    lax.fori_loop(1, 32, ask, 0)
    req_in[tab] = req_out[tab]

    slot = owner * 16 + rank.astype(jnp.int32)
    first_half = lax.broadcasted_iota(jnp.int32, (1, TOK), 1) < SEQ
    for p in range(PAIRS):
        a = slot[2 * p : 2 * p + 1, :]
        b = slot[2 * p + 1 : 2 * p + 2, :] + MOST
        item = jnp.where(first_half, a, pltpu.roll(b, SEQ, 1))
        action = jnp.where(first_half, pltpu.roll(a, SEQ, 1), b)
        length = jnp.where(first_half, lengths[2 * p : 2 * p + 1], lengths[2 * p + 1 : 2 * p + 2])
        block = jnp.concatenate([item, action, length, length] * 2, axis=0)
        rows_s[p] = block
        cols_s[p] = block.astype(F32).T.astype(jnp.int32)

    def asked(k, carry):
        req_copy(k).wait_recv()
        return carry

    lax.fori_loop(1, 32, asked, 0)
    asks = jnp.concatenate([req_in[k] for k in range(N_TABLE)], axis=0)
    low, high = split_number(asks)
    tall = lax.broadcasted_iota(jnp.int32, (SLOTS, N_TABLE), 0) // 16
    tall = (tall == lax.broadcasted_iota(jnp.int32, (SLOTS, N_TABLE), 1)).astype(BF16)
    wanted[...] = mm(tall, low) + 256.0 * mm(tall, high) - 1.0
    wide = lax.broadcasted_iota(jnp.int32, (N_TABLE, SLOTS), 1) // 16
    wide = (wide == lax.broadcasted_iota(jnp.int32, (N_TABLE, SLOTS), 0)).astype(BF16)
    across = mm_tn(low, wide) + 256.0 * mm_tn(high, wide) - 1.0
    at = lax.broadcasted_iota(jnp.int32, (TOK, SLOTS), 0)
    in_owner = lax.broadcasted_iota(jnp.int32, (TOK, SLOTS), 1) % 16
    for p in range(PAIRS):
        line = jnp.sum(jnp.where(at == in_owner + 16 * p, across, 0.0), axis=0, keepdims=True)
        req_rows[:, p * SLOTS : (p + 1) * SLOTS] = line.astype(jnp.int32)

    def fetch_copy(p, k):
        peer = lax.rem(tab + k, 32)
        return pltpu.make_async_remote_copy(
            src_ref=picked.at[p, peer], dst_ref=replies.at[p, tab],
            send_sem=f_send.at[p, k], recv_sem=f_recv.at[p, k],
            device_id=(dp, peer), device_id_type=MESH,
        )

    loads[0].wait()

    def serve(p, carry):
        at = lax.broadcasted_iota(jnp.int32, (SLOTS, TOK), 0) % 16 + 16 * p
        seen = lax.broadcasted_iota(jnp.int32, (SLOTS, TOK), 1) == at
        line = jnp.sum(jnp.where(seen, wanted[...], 0.0), axis=1, keepdims=True)
        line = line.astype(jnp.int32)
        places = lax.broadcasted_iota(jnp.int32, (SLOTS, ROWS_DEV), 1)
        chosen = (places == line).astype(BF16)
        picked[p] = mm(chosen, table[...]).astype(BF16).reshape(N_TABLE, 16, EMB)

        def start(k, inner):
            fetch_copy(p, k).start()
            return inner

        lax.fori_loop(1, 32, start, 0)
        replies[p, tab] = picked[p, tab]
        return carry

    lax.fori_loop(0, PAIRS, serve, 0)

    def give_copy(p, k):
        peer = lax.rem(tab + k, 32)
        return pltpu.make_async_remote_copy(
            src_ref=outgoing.at[p, peer], dst_ref=incoming.at[p, tab],
            send_sem=a_send.at[p, k], recv_sem=a_recv.at[p, k],
            device_id=(dp, peer), device_id_type=MESH,
        )

    for load in loads[1:]:
        load.wait()

    def pair(p, carry):
        def landed(k, inner):
            fetch_copy(p, k).wait_recv()
            return inner

        lax.fori_loop(1, 32, landed, 0)
        tokens = pl.ds(pl.multiple_of(p * TOK, TOK), TOK)
        normed_p, mixed_p, top_p, before_p, back = layer_pair(
            replies[p].reshape(SLOTS, EMB), cols_s[p], rows_s[p], up[tokens, :], wp, wo
        )
        outgoing[p] = back.reshape(N_TABLE, 16, EMB)

        def start(k, inner):
            give_copy(p, k).start()
            return inner

        lax.fori_loop(1, 32, start, 0)
        incoming[p, tab] = outgoing[p, tab]
        normed_t[:, tokens] = normed_p
        mixed_t[:, tokens] = mixed_p
        tops[tokens, :] = top_p
        gbs[tokens, :] = before_p
        return carry

    lax.fori_loop(0, PAIRS, pair, 0)

    def core_copy(k):
        return pltpu.make_async_remote_copy(
            src_ref=g.at[0, k], dst_ref=core_buf.at[k],
            send_sem=core_send.at[k], recv_sem=core_recv.at[k],
            device_id=other, device_id_type=MESH,
        )

    def terms(k, carry):
        first = mm(normed_t[...], gbs[:, pl.ds(pl.multiple_of(k * 768, 768), 768)]) * SCALE
        second = mm(mixed_t[...], tops[:, pl.ds(pl.multiple_of(k * 256, 256), 256)]) * SCALE
        for which, kept in ((0, 1 - c), (1, c)):
            one = first[:, which * 384 : (which + 1) * 384].astype(BF16)
            two = second[:, which * 128 : (which + 1) * 128].astype(BF16)
            g[kept, k, :, :, 0:384] = one.reshape(4, 256, 384)
            g[kept, k, :, :, 384:512] = two.reshape(4, 256, 128)
        core_copy(k).start()
        return carry

    lax.fori_loop(0, 4, terms, 0)
    s1 = g.at[1]

    def merge(k, carry):
        core_copy(k).wait_recv()

        def step(n, inner):
            s1[k, n] = (s1[k, n].astype(F32) + core_buf[k, n].astype(F32)).astype(BF16)
            return inner

        lax.fori_loop(0, 4, step, 0)
        return carry

    lax.fori_loop(0, 4, merge, 0)

    def two(ref, n):
        return ref.at[pl.ds(2 * n, 2)]

    ring_a = Ring(y, y_right, y_left, lambda k: s1.at[k, :, pl.ds(0, 128), :], two, far_a, near_a,
                  ring_send.at[0], ring_recv.at[0])
    ring_b = Ring(x, x_right, x_left, lambda k: s1.at[:, k, pl.ds(128, 128), :], two, far_b, near_b,
                  ring_send.at[1], ring_recv.at[1])
    ring_a.begin()
    ring_b.begin()
    ring_a.forward(add_into)
    ring_b.forward(add_into)
    ring_a.arrive()
    for n in range(4):
        sum_a[n] = (
            s1[y, n, 0:128, :].astype(F32) + near_a[0, n].astype(F32) + near_a[1, n].astype(F32)
        ).astype(BF16)

    def rows64(ref, n):
        return ref.at[pl.ds(64 * n, 64), :]

    def add_flat(target, other_ref):
        target[...] = (target[...].astype(F32) + other_ref[...].astype(F32)).astype(BF16)

    ring_a2 = Ring(x, x_right, x_left, lambda k: sum_a.at[k], rows64, far_a2, near_a2,
                   ring_send.at[2], ring_recv.at[2])
    ring_a2.begin()
    ring_b.arrive()
    for n in range(4):
        sum_b[n] = (
            s1[n, x, 128:256, :].astype(F32) + near_b[0, n].astype(F32) + near_b[1, n].astype(F32)
        ).astype(BF16)
    ring_b2 = Ring(y, y_right, y_left, lambda k: sum_b.at[k], rows64, far_b2, near_b2,
                   ring_send.at[3], ring_recv.at[3])
    ring_b2.begin()
    ring_a2.forward(add_flat)
    ring_b2.forward(add_flat)
    ring_a2.arrive()
    total = sum_a[x].astype(F32) + near_a2[0].astype(F32) + near_a2[1].astype(F32)
    s4[0:4] = total.astype(BF16).reshape(4, 32, 512)
    ring_b2.arrive()
    total = sum_b[y].astype(F32) + near_b2[0].astype(F32) + near_b2[1].astype(F32)
    s4[4:8] = total.astype(BF16).reshape(4, 32, 512)

    def z_copy(k):
        peer = lax.rem(z + k, 8)
        return pltpu.make_async_remote_copy(
            src_ref=s4.at[peer], dst_ref=zbuf.at[k],
            send_sem=z_send.at[k], recv_sem=z_recv.at[k],
            device_id=(dp, 8 * x + peer), device_id_type=MESH,
        )

    for k in range(1, 8):
        z_copy(k).start()

    def given(n, carry):
        give_copy(n // 31, n % 31 + 1).wait_recv()
        return carry

    lax.fori_loop(0, PAIRS * 31, given, 0)

    def rows_of(first):
        places = lax.broadcasted_iota(jnp.int32, (256, ROWS_DEV), 0) + first
        chosen = (places == req_rows[...]).astype(BF16)
        return mm(chosen, incoming[...].reshape(PAIRS * SLOTS, EMB)).astype(BF16).astype(F32)

    def table_block(b, carry):
        upper = rows_of(b * 256)
        lower = rows_of(b * 256 + 1024)
        rows = pl.ds(pl.multiple_of(b * 256, 256), 256)
        is_left = lax.broadcasted_iota(jnp.int32, (256, 128), 1) < 64
        for k in range(4):
            up_k, low_k = upper[:, k * 128 : (k + 1) * 128], lower[:, k * 128 : (k + 1) * 128]
            t2[0, k, rows, :] = jnp.where(is_left, up_k, pltpu.roll(low_k, 64, 1)).astype(BF16)
            t2[1, k, rows, :] = jnp.where(is_left, pltpu.roll(up_k, 64, 1), low_k).astype(BF16)
        return carry

    lax.fori_loop(0, 4, table_block, 0)
    t_copy = pltpu.make_async_remote_copy(
        src_ref=t2.at[1 - c], dst_ref=t_core, send_sem=core_send.at[4], recv_sem=core_recv.at[4],
        device_id=other, device_id_type=MESH,
    )
    t_copy.start()

    total = s4[z].astype(F32)
    for k in range(1, 8):
        z_copy(k).wait_recv()
        total = total + zbuf[k].astype(F32)
    total = total.astype(BF16)
    proj_ref[...] = total[:, :384]
    outw_ref[...] = total[:, 384:]

    t_copy.wait_recv()
    for k in range(4):
        add_flat(t2.at[c, k], t_core.at[k])

    def rows512(ref, n):
        return ref.at[pl.ds(512 * n, 512), :]

    ring_t = Ring(y, y_right, y_left, lambda k: t2.at[c, k], rows512, t_far, t_near,
                  ring_send.at[4], ring_recv.at[4])
    ring_t.begin()
    ring_t.forward(add_flat)
    ring_t.arrive()
    total = t2[c, y].astype(F32) + t_near[0].astype(F32) + t_near[1].astype(F32)
    total = total.T.astype(BF16)
    table_ref[:, 0:1024] = total[0:64]
    table_ref[:, 1024:2048] = total[64:128]

    def sent(k, carry):
        req_copy(k).wait_send()
        for p in range(PAIRS):
            fetch_copy(p, k).wait_send()
            give_copy(p, k).wait_send()
        return carry

    lax.fori_loop(1, 32, sent, 0)
    for k in range(4):
        core_copy(k).wait_send()
    for k in range(1, 8):
        msg_copy(k).wait_send()
        z_copy(k).wait_send()
    t_copy.wait_send()
    for ring in (ring_a, ring_b, ring_a2, ring_b2, ring_t):
        ring.end()


def run(message, order, table, upstream, proj_weight, out_weight):
    whole = pl.BlockSpec(memory_space=pltpu.VMEM)
    anywhere = pl.BlockSpec(memory_space=pl.ANY)
    dma = pltpu.SemaphoreType.DMA
    tokens = HIST * SEQ

    def buf(*shape):
        return pltpu.VMEM(shape, BF16)

    return pl.pallas_call(
        program_kernel,
        out_shape=(
            jax.ShapeDtypeStruct((32, 384), BF16),
            jax.ShapeDtypeStruct((32, 128), BF16),
            jax.ShapeDtypeStruct((64, 2048), BF16),
        ),
        in_specs=[whole] * 2 + [anywhere] * 4,
        out_specs=(whole,) * 3,
        scratch_shapes=[
            buf(ROWS_DEV, EMB), buf(tokens, D), buf(D, PROJ), buf(D, D),
            pltpu.VMEM((HIST, 1, 256), jnp.int32),
            pltpu.VMEM((HIST, 1, 256), jnp.int32),
            pltpu.VMEM((N_TABLE, 1, TOK), jnp.int32),
            pltpu.VMEM((N_TABLE, 1, TOK), jnp.int32),
            pltpu.VMEM((SLOTS, TOK), F32),
            pltpu.VMEM((1, PAIRS * SLOTS), jnp.int32),
            pltpu.VMEM((PAIRS, 8, TOK), jnp.int32),
            pltpu.VMEM((PAIRS, TOK, 8), jnp.int32),
            buf(PAIRS, N_TABLE, 16, EMB), buf(PAIRS, N_TABLE, 16, EMB),
            buf(PAIRS, N_TABLE, 16, EMB), buf(PAIRS, N_TABLE, 16, EMB),
            buf(D, tokens), buf(D, tokens), buf(tokens, D), buf(tokens, PROJ),
            buf(2, 4, 4, 256, 512), buf(4, 4, 256, 512),
            buf(2, 2, 128, 512), buf(2, 2, 128, 512), buf(2, 4, 128, 512), buf(2, 4, 128, 512),
            buf(4, 128, 512), buf(4, 128, 512),
            buf(2, 64, 512), buf(2, 64, 512), buf(2, 128, 512), buf(2, 128, 512),
            buf(8, 32, 512), buf(8, 32, 512),
            buf(2, 4, 1024, 128), buf(4, 1024, 128), buf(2, 512, 128), buf(2, 1024, 128),
            dma((4,)), dma((8,)), dma((8,)), dma((32,)), dma((32,)),
            dma((PAIRS, 32)), dma((PAIRS, 32)), dma((PAIRS, 32)), dma((PAIRS, 32)),
            dma((5,)), dma((5,)), dma((5, 6)), dma((5, 6)), dma((8,)), dma((8,)),
        ],
        compiler_params=pltpu.CompilerParams(
            vmem_limit_bytes=VMEM_LIMIT, collective_id=0, has_side_effects=True
        ),
        name="whole_program",
    )(message, order, table, upstream, proj_weight, out_weight)


def body(
    embed_table, owner_shard, slot_row, lengths, send_order, proj_weight, out_weight, upstream
):
    ids = owner_shard[..., 0] * ROWS_DEV + slot_row
    ids = jnp.swapaxes(ids, 1, 2).reshape(HIST, 2 * SEQ)
    lengths = jnp.broadcast_to(lengths[:, None], (HIST, 2 * SEQ))
    message = jnp.concatenate([ids, lengths], axis=1)
    proj, outw, table = run(
        message, send_order.reshape(HIST, 1), embed_table, upstream.reshape(HIST * SEQ, D),
        proj_weight, out_weight,
    )
    return table.T, proj, outw


def solution(mesh):
    in_specs = (
        P("table", None),
        P(("dp", "table"), None, None, None),
        P(("dp", "table"), None, None),
        P(("dp", "table")),
        P(("dp", "table"), None),
        P(),
        P(),
        P(("dp", "table"), None, None),
    )
    out_specs = (P("table", "dp"), P("table", "dp"), P("table", "dp"))
    return jax.shard_map(body, mesh=mesh, in_specs=in_specs, out_specs=out_specs, check_vma=False)
```

time: 233 us -> 162 us (0.70)
  waiting for transfers between devices: 50.9 us -> 0 us
  Pallas kernels: 134 us -> 153 us
  blocking collectives: 19 us -> 0 us
  starting transfers between devices: 10.7 us -> 0 us
  local copies, waits for them, and re-layouts: 13.5 us -> 6.44 us
    all_to_all x2 -> x0, waiting for transfers between devices: 50.9 us -> none  [the longest x1 46.4 us: body(): lax.all_to_all(picked, 'table', split_axis=0, concat_axis=0, tiled=True)]
    all_to_all x1 -> x0, blocking collectives: 19 us -> none  [body(): lax.all_to_all(request, 'table', split_axis=0, concat_axis=0, tiled=True)]
    pallas_call x3 -> x1, Pallas kernels: 134 us -> 153 us  [run(): pl.pallas_call(program_kernel, out_shape=(jax.ShapeDtypeStruct((32, 384),...]
    all_to_all x2 -> x0, starting transfers between devices: 10.7 us -> none  [the longest x1 6.48 us: body(): lax.all_to_all(message, 'dp', split_axis=0, concat_axis=0, tiled=True)]
    slice x5 -> x0, local copies, waits for them, and re-layouts: 3.93 us -> none  [the longest x2 2.64 us: body(): return (table, dense[:, :384], dense[:, 384:])]
  transfers between devices with their start and end apart: 2 -> 0, of which waited for: 2 -> 0; matrix products, arithmetic and copies ran while one was open for 1% -> 0% of each run, Pallas kernels for 0% -> 0%
where the time goes in v2:
time: 162 us; the launch traced here: 161 us
  Pallas kernels  153 us (94%)
  local copies, waits for them, and re-layouts  6.44 us (4%)
    pallas_call x1, Pallas kernels, run(): pl.pallas_call(program_kernel, out_shape=(jax.ShapeDtypeStruct((32, 384),...  153 us
    unnamed x3, local copies, waits for them, and re-layouts  4.31 us

profile of v2, /device:TPU:1, one launch (start us, length us, event | category | flops | bytes accessed | tf_op | source)
XLA Modules:
  0.0 161.4 jit_solution(12562792143771571299)
XLA Ops:
  0.6 0.7 broadcast_in_dim.2
  1.4 1.3 copy.12.order_ref
  2.7 0.7 fusion
  3.4 0.1 reshape.18
  3.5 0.6 pad_add_fusion.msg_ref
  4.1 153.0 %whole_program.1 = (bf16[32,384]{1,0:T(8,128)(2,1)}, bf16[32,128]{1,0:T(8,128)(2,1)}, bf16[64,2048]{1,0:T(8,128)(2,1)}) custom-call(s32[8,256]{1,0:T(8,128)} %pad_add_fusion.msg_ref, s32[8,1]{1,0:T(8,128)} %copy.12.order_ref, bf16[2048,512]{1,0:T(8,128)(2,1)} %table_hbm.1, bf16[512,1024]{1,0:T(8,128)(2,1)} %bitcast.10, bf16[1024,3072]{1,0:T(8,128)(2,1)} %wp_hbm.1, ...), custom_call_target="tpu_custom_call" | custom-call | tf_op jit(solution)/shard_map/whole_program/pallas_call | solution.py:563
  157.1 1.7 %copy.16 = bf16[2048,64]{0,1:T(8,128)(2,1)} copy(bf16[2048,64]{0,1:T(8,128)(2,1)} %bitcast.11) | data formatting | bytes 524288
  158.7 1.3 copy.17
  160.1 1.3 copy.18

commit v3 on v2

--- a/solution.py
+++ b/solution.py
@@ -25,6 +25,7 @@
 SCALE = float(2048 * 64) ** (-0.5)
 MESH = pl.DeviceIdType.MESH
 VMEM_LIMIT = 60 * 1024 * 1024
+CUT = 160
 F32 = jnp.float32
 BF16 = jnp.bfloat16
 
@@ -57,7 +58,7 @@
             device_id=device, device_id_type=MESH,
         )
 
-    def begin(self):
+    def make(self):
         across, after, ahead = (lax.rem(self.place + k, 4) for k in (2, 1, 3))
         self.after, self.ahead = after, ahead
         part, half, far, near = self.chunk, self.half, self.far, self.near
@@ -69,8 +70,14 @@
             self.copy(4, half(part(after), 0), half(near.at[0], 0), self.right),
             self.copy(5, half(part(ahead), 1), half(near.at[1], 1), self.left),
         ]
-        for k in range(4):
+
+    def start_half(self, number):
+        for k in ((0, 3), (1, 2))[number]:
             self.copies[k].start()
+
+    def start(self):
+        self.start_half(0)
+        self.start_half(1)
 
     def forward(self, add):
         self.copies[0].wait_recv()
@@ -185,12 +192,12 @@
 
 
 def program_kernel(
-    msg_ref, order_ref, table_hbm, up_hbm, wp_hbm, wo_hbm,
-    proj_ref, outw_ref, table_ref,
+    owner_ref, slot_ref, length_ref, order_ref, table_hbm, up_hbm, wp_hbm, wo_hbm,
+    dense_ref, table_ref,
     table, up, wp, wo, msg_out, msg_in, req_out, req_in, wanted, req_rows, rows_s, cols_s,
-    picked, replies, outgoing, incoming, normed_t, mixed_t, tops, gbs,
-    g, core_buf, far_a, far_b, near_a, near_b, sum_a, sum_b,
-    far_a2, far_b2, near_a2, near_b2, s4, zbuf, t2, t_core, t_far, t_near,
+    picked, replies, incoming, normed_t, mixed_t, gbs,
+    g, core_buf, sums, far_a, far_b, near_a, near_b, sum_a, sum_b,
+    far_a2, far_b2, near_a2, near_b2, s4, zbuf, t_core, t_far, t_near,
     load_sem, m_send, m_recv, r_send, r_recv, f_send, f_recv, a_send, a_recv,
     core_send, core_recv, ring_send, ring_recv, z_send, z_recv,
 ):
@@ -231,11 +238,16 @@
     lax.fori_loop(1, 32, greet_table, 0)
 
     order = order_ref[...]
-    message = jnp.zeros((HIST, 256), jnp.int32)
-    for m in range(HIST):
-        message = message + jnp.where(order == m, msg_ref[m : m + 1, :], 0)
+    rows_of_table = [owner_ref[m] * ROWS_DEV + slot_ref[m] for m in range(HIST)]
     for k in range(HIST):
-        msg_out[k] = message[k : k + 1, :]
+        at = order[:, k : k + 1]
+        lookups = jnp.zeros((2, SEQ), jnp.int32)
+        length = jnp.zeros((1, 1), jnp.int32)
+        for m in range(HIST):
+            lookups = jnp.where(jnp.broadcast_to(at, (2, SEQ)) == m, rows_of_table[m], lookups)
+            length = jnp.where(at == m, length_ref[:, m : m + 1], length)
+        msg_out[k, 0:2, 0:SEQ] = lookups
+        msg_out[k, 2:3, 0:SEQ] = jnp.broadcast_to(length, (1, SEQ))
     pl.semaphore_wait(barrier, 38)
 
     def msg_copy(k):
@@ -252,8 +264,11 @@
     for k in range(1, 8):
         msg_copy(k).wait_recv()
 
-    got = jnp.concatenate([msg_in[k] for k in range(HIST)], axis=0)
-    ids, lengths = got[:, : 2 * SEQ], got[:, 2 * SEQ : 2 * SEQ + 1]
+    items = jnp.concatenate([msg_in[k, 0:1, :] for k in range(HIST)], axis=0)
+    actions = jnp.concatenate([msg_in[k, 1:2, :] for k in range(HIST)], axis=0)
+    lengths = jnp.concatenate([msg_in[k, 2:3, :] for k in range(HIST)], axis=0)[:, 0:1]
+    is_item = lax.broadcasted_iota(jnp.int32, (HIST, TOK), 1) < SEQ
+    ids = jnp.where(is_item, items, pltpu.roll(actions, SEQ, 1))
     owner = ids // ROWS_DEV
     ids_col = ids.astype(F32).T.astype(jnp.int32)
     owner_col, row_col = ids_col // ROWS_DEV, ids_col % ROWS_DEV
@@ -355,6 +370,8 @@
 
     lax.fori_loop(0, PAIRS, serve, 0)
 
+    outgoing = picked
+
     def give_copy(p, k):
         peer = lax.rem(tab + k, 32)
         return pltpu.make_async_remote_copy(
@@ -366,31 +383,39 @@
     for load in loads[1:]:
         load.wait()
 
+    def give(n, carry):
+        give_copy(n // 31, n % 31 + 1).start()
+        return carry
+
+    def fetched(p):
+        def landed(k, carry):
+            fetch_copy(p, k).wait_recv()
+            fetch_copy(p, k).wait_send()
+            return carry
+
+        lax.fori_loop(1, 32, landed, 0)
+
     def pair(p, carry):
-        def landed(k, inner):
-            fetch_copy(p, k).wait_recv()
-            return inner
-
-        lax.fori_loop(1, 32, landed, 0)
+        fetched(p)
+
+        @pl.when(p == PAIRS - 1)
+        def _():
+            lax.fori_loop(0, (PAIRS - 1) * 31, give, 0)
+
         tokens = pl.ds(pl.multiple_of(p * TOK, TOK), TOK)
         normed_p, mixed_p, top_p, before_p, back = layer_pair(
             replies[p].reshape(SLOTS, EMB), cols_s[p], rows_s[p], up[tokens, :], wp, wo
         )
         outgoing[p] = back.reshape(N_TABLE, 16, EMB)
-
-        def start(k, inner):
-            give_copy(p, k).start()
-            return inner
-
-        lax.fori_loop(1, 32, start, 0)
         incoming[p, tab] = outgoing[p, tab]
         normed_t[:, tokens] = normed_p
         mixed_t[:, tokens] = mixed_p
-        tops[tokens, :] = top_p
+        up[tokens, :] = top_p
         gbs[tokens, :] = before_p
         return carry
 
     lax.fori_loop(0, PAIRS, pair, 0)
+    lax.fori_loop((PAIRS - 1) * 31, PAIRS * 31, give, 0)
 
     def core_copy(k):
         return pltpu.make_async_remote_copy(
@@ -401,7 +426,7 @@
 
     def terms(k, carry):
         first = mm(normed_t[...], gbs[:, pl.ds(pl.multiple_of(k * 768, 768), 768)]) * SCALE
-        second = mm(mixed_t[...], tops[:, pl.ds(pl.multiple_of(k * 256, 256), 256)]) * SCALE
+        second = mm(mixed_t[...], up[:, pl.ds(pl.multiple_of(k * 256, 256), 256)]) * SCALE
         for which, kept in ((0, 1 - c), (1, c)):
             one = first[:, which * 384 : (which + 1) * 384].astype(BF16)
             two = second[:, which * 128 : (which + 1) * 128].astype(BF16)
@@ -412,9 +437,11 @@
 
     lax.fori_loop(0, 4, terms, 0)
     s1 = g.at[1]
+    t2 = g.at[0]
 
     def merge(k, carry):
         core_copy(k).wait_recv()
+        core_copy(k).wait_send()
 
         def step(n, inner):
             s1[k, n] = (s1[k, n].astype(F32) + core_buf[k, n].astype(F32)).astype(BF16)
@@ -428,45 +455,72 @@
     def two(ref, n):
         return ref.at[pl.ds(2 * n, 2)]
 
-    ring_a = Ring(y, y_right, y_left, lambda k: s1.at[k, :, pl.ds(0, 128), :], two, far_a, near_a,
+    def add_flat(target, other_ref):
+        target[...] = (target[...].astype(F32) + other_ref[...].astype(F32)).astype(BF16)
+
+    def chosen_rows(p, first, count):
+        places = lax.broadcasted_iota(jnp.int32, (count, SLOTS), 0) + first
+        return (places == req_rows[:, p * SLOTS : (p + 1) * SLOTS]).astype(BF16)
+
+    def take_in(p):
+        def given(k, carry):
+            give_copy(p, k).wait_recv()
+            return carry
+
+        lax.fori_loop(1, 32, given, 0)
+
+    def add_rows(p):
+        take_in(p)
+
+        def block(b, carry):
+            first = b * 512
+            part = mm(chosen_rows(p, first, 512), incoming[p].reshape(SLOTS, EMB))
+            rows = pl.ds(pl.multiple_of(first, 512), 512)
+            sums[rows, :] = part if p == 0 else sums[rows, :] + part
+            return carry
+
+        lax.fori_loop(0, 4, block, 0)
+
+    ring_a = Ring(y, y_right, y_left, lambda k: s1.at[k, :, pl.ds(0, CUT), :], two, far_a, near_a,
                   ring_send.at[0], ring_recv.at[0])
-    ring_b = Ring(x, x_right, x_left, lambda k: s1.at[:, k, pl.ds(128, 128), :], two, far_b, near_b,
-                  ring_send.at[1], ring_recv.at[1])
-    ring_a.begin()
-    ring_b.begin()
+    ring_b = Ring(x, x_right, x_left, lambda k: s1.at[:, k, pl.ds(CUT, 256 - CUT), :], two, far_b,
+                  near_b, ring_send.at[1], ring_recv.at[1])
+    for ring in (ring_a, ring_b):
+        ring.make()
+        ring.start()
+    add_rows(0)
     ring_a.forward(add_into)
     ring_b.forward(add_into)
+    add_rows(1)
+    ring_b.arrive()
+    for n in range(4):
+        sum_b[n] = (
+            s1[n, x, CUT:256, :].astype(F32) + near_b[0, n].astype(F32) + near_b[1, n].astype(F32)
+        ).astype(BF16)
+    ring_b2 = Ring(y, y_right, y_left, lambda k: sum_b.at[k],
+                   lambda ref, n: ref.at[pl.ds((256 - CUT) // 2 * n, (256 - CUT) // 2), :],
+                   far_b2, near_b2, ring_send.at[3], ring_recv.at[3])
+    ring_b2.make()
+    ring_b2.start()
     ring_a.arrive()
     for n in range(4):
         sum_a[n] = (
-            s1[y, n, 0:128, :].astype(F32) + near_a[0, n].astype(F32) + near_a[1, n].astype(F32)
+            s1[y, n, 0:CUT, :].astype(F32) + near_a[0, n].astype(F32) + near_a[1, n].astype(F32)
         ).astype(BF16)
-
-    def rows64(ref, n):
-        return ref.at[pl.ds(64 * n, 64), :]
-
-    def add_flat(target, other_ref):
-        target[...] = (target[...].astype(F32) + other_ref[...].astype(F32)).astype(BF16)
-
-    ring_a2 = Ring(x, x_right, x_left, lambda k: sum_a.at[k], rows64, far_a2, near_a2,
+    ring_a2 = Ring(x, x_right, x_left, lambda k: sum_a.at[k],
+                   lambda ref, n: ref.at[pl.ds(CUT // 2 * n, CUT // 2), :], far_a2, near_a2,
                    ring_send.at[2], ring_recv.at[2])
-    ring_a2.begin()
-    ring_b.arrive()
-    for n in range(4):
-        sum_b[n] = (
-            s1[n, x, 128:256, :].astype(F32) + near_b[0, n].astype(F32) + near_b[1, n].astype(F32)
-        ).astype(BF16)
-    ring_b2 = Ring(y, y_right, y_left, lambda k: sum_b.at[k], rows64, far_b2, near_b2,
-                   ring_send.at[3], ring_recv.at[3])
-    ring_b2.begin()
+    ring_a2.make()
+    ring_a2.start()
+    ring_b2.forward(add_flat)
     ring_a2.forward(add_flat)
-    ring_b2.forward(add_flat)
+    add_rows(2)
+    ring_b2.arrive()
+    total = sum_b[y].astype(F32) + near_b2[0].astype(F32) + near_b2[1].astype(F32)
+    s4[CUT // 32 : 8] = total.astype(BF16).reshape(8 - CUT // 32, 32, 512)
     ring_a2.arrive()
     total = sum_a[x].astype(F32) + near_a2[0].astype(F32) + near_a2[1].astype(F32)
-    s4[0:4] = total.astype(BF16).reshape(4, 32, 512)
-    ring_b2.arrive()
-    total = sum_b[y].astype(F32) + near_b2[0].astype(F32) + near_b2[1].astype(F32)
-    s4[4:8] = total.astype(BF16).reshape(4, 32, 512)
+    s4[0 : CUT // 32] = total.astype(BF16).reshape(CUT // 32, 32, 512)
 
     def z_copy(k):
         peer = lax.rem(z + k, 8)
@@ -479,79 +533,90 @@
     for k in range(1, 8):
         z_copy(k).start()
 
-    def given(n, carry):
-        give_copy(n // 31, n % 31 + 1).wait_recv()
-        return carry
-
-    lax.fori_loop(0, PAIRS * 31, given, 0)
+    take_in(PAIRS - 1)
 
     def rows_of(first):
-        places = lax.broadcasted_iota(jnp.int32, (256, ROWS_DEV), 0) + first
-        chosen = (places == req_rows[...]).astype(BF16)
-        return mm(chosen, incoming[...].reshape(PAIRS * SLOTS, EMB)).astype(BF16).astype(F32)
+        part = mm(chosen_rows(PAIRS - 1, first, 256), incoming[PAIRS - 1].reshape(SLOTS, EMB))
+        rows = pl.ds(pl.multiple_of(first, 256), 256)
+        return (sums[rows, :] + part).astype(BF16).astype(F32)
+
+    def t_copy(b):
+        lanes = pl.ds(pl.multiple_of(b * 128, 128), 128)
+        return pltpu.make_async_remote_copy(
+            src_ref=t2.at[1 - c, :, :, lanes], dst_ref=t_core.at[:, :, lanes],
+            send_sem=core_send.at[4 + b], recv_sem=core_recv.at[4 + b],
+            device_id=other, device_id_type=MESH,
+        )
 
     def table_block(b, carry):
         upper = rows_of(b * 256)
         lower = rows_of(b * 256 + 1024)
-        rows = pl.ds(pl.multiple_of(b * 256, 256), 256)
+        lanes = pl.ds(pl.multiple_of(b * 128, 128), 128)
         is_left = lax.broadcasted_iota(jnp.int32, (256, 128), 1) < 64
         for k in range(4):
             up_k, low_k = upper[:, k * 128 : (k + 1) * 128], lower[:, k * 128 : (k + 1) * 128]
-            t2[0, k, rows, :] = jnp.where(is_left, up_k, pltpu.roll(low_k, 64, 1)).astype(BF16)
-            t2[1, k, rows, :] = jnp.where(is_left, pltpu.roll(up_k, 64, 1), low_k).astype(BF16)
-        return carry
-
-    lax.fori_loop(0, 4, table_block, 0)
-    t_copy = pltpu.make_async_remote_copy(
-        src_ref=t2.at[1 - c], dst_ref=t_core, send_sem=core_send.at[4], recv_sem=core_recv.at[4],
-        device_id=other, device_id_type=MESH,
-    )
-    t_copy.start()
+            t2[0, k, :, lanes] = jnp.where(is_left, up_k, pltpu.roll(low_k, 64, 1)).astype(BF16)
+            t2[1, k, :, lanes] = jnp.where(is_left, pltpu.roll(up_k, 64, 1), low_k).astype(BF16)
+        t_copy(b).start()
+        return carry
+
+    def table_merge(b, carry):
+        t_copy(b).wait_recv()
+        lanes = pl.ds(pl.multiple_of(b * 128, 128), 128)
+        for k in range(4):
+            mine = t2[c, k, :, lanes].astype(F32) + t_core[k, :, lanes].astype(F32)
+            t2[c, k, :, lanes] = mine.astype(BF16)
+        return carry
+
+    ring_t = Ring(y, y_right, y_left, lambda k: t2.at[c, k],
+                  lambda ref, n: ref.at[:, pl.ds(256 * n, 256)], t_far, t_near,
+                  ring_send.at[4], ring_recv.at[4])
+    ring_t.make()
+    lax.fori_loop(0, 3, table_block, 0)
+    lax.fori_loop(0, 2, table_merge, 0)
+    ring_t.start_half(0)
+    lax.fori_loop(3, 4, table_block, 0)
+    lax.fori_loop(2, 4, table_merge, 0)
+    ring_t.start_half(1)
 
     total = s4[z].astype(F32)
     for k in range(1, 8):
         z_copy(k).wait_recv()
         total = total + zbuf[k].astype(F32)
-    total = total.astype(BF16)
-    proj_ref[...] = total[:, :384]
-    outw_ref[...] = total[:, 384:]
-
-    t_copy.wait_recv()
-    for k in range(4):
-        add_flat(t2.at[c, k], t_core.at[k])
-
-    def rows512(ref, n):
-        return ref.at[pl.ds(512 * n, 512), :]
-
-    ring_t = Ring(y, y_right, y_left, lambda k: t2.at[c, k], rows512, t_far, t_near,
-                  ring_send.at[4], ring_recv.at[4])
-    ring_t.begin()
+    dense_ref[...] = total.astype(BF16)
+
     ring_t.forward(add_flat)
     ring_t.arrive()
     total = t2[c, y].astype(F32) + t_near[0].astype(F32) + t_near[1].astype(F32)
-    total = total.T.astype(BF16)
-    table_ref[:, 0:1024] = total[0:64]
-    table_ref[:, 1024:2048] = total[64:128]
+    table_ref[...] = total.astype(BF16)
 
     def sent(k, carry):
         req_copy(k).wait_send()
         for p in range(PAIRS):
-            fetch_copy(p, k).wait_send()
             give_copy(p, k).wait_send()
         return carry
 
     lax.fori_loop(1, 32, sent, 0)
     for k in range(4):
-        core_copy(k).wait_send()
+        t_copy(k).wait_send()
     for k in range(1, 8):
         msg_copy(k).wait_send()
         z_copy(k).wait_send()
-    t_copy.wait_send()
     for ring in (ring_a, ring_b, ring_a2, ring_b2, ring_t):
         ring.end()
 
 
-def run(message, order, table, upstream, proj_weight, out_weight):
+def output_kernel(dense_ref, sums_ref, proj_ref, outw_ref, table_ref):
+    proj_ref[...] = dense_ref[:, :384]
+    outw_ref[...] = dense_ref[:, 384:]
+    across = sums_ref[...].astype(F32).T.astype(BF16)
+    for b in range(4):
+        for half in range(2):
+            part = across[b * 128 + half * 64 : b * 128 + half * 64 + 64]
+            table_ref[:, half * 1024 + b * 256 : half * 1024 + (b + 1) * 256] = part
+
+
+def run(*arrays):
     whole = pl.BlockSpec(memory_space=pltpu.VMEM)
     anywhere = pl.BlockSpec(memory_space=pl.ANY)
     dma = pltpu.SemaphoreType.DMA
@@ -560,19 +625,18 @@
     def buf(*shape):
         return pltpu.VMEM(shape, BF16)
 
-    return pl.pallas_call(
+    parts = pl.pallas_call(
         program_kernel,
         out_shape=(
-            jax.ShapeDtypeStruct((32, 384), BF16),
-            jax.ShapeDtypeStruct((32, 128), BF16),
-            jax.ShapeDtypeStruct((64, 2048), BF16),
+            jax.ShapeDtypeStruct((32, 512), BF16),
+            jax.ShapeDtypeStruct((256, 512), BF16),
         ),
-        in_specs=[whole] * 2 + [anywhere] * 4,
-        out_specs=(whole,) * 3,
+        in_specs=[whole] * 4 + [anywhere] * 4,
+        out_specs=(whole,) * 2,
         scratch_shapes=[
             buf(ROWS_DEV, EMB), buf(tokens, D), buf(D, PROJ), buf(D, D),
-            pltpu.VMEM((HIST, 1, 256), jnp.int32),
-            pltpu.VMEM((HIST, 1, 256), jnp.int32),
+            pltpu.VMEM((HIST, 8, TOK), jnp.int32),
+            pltpu.VMEM((HIST, 8, TOK), jnp.int32),
             pltpu.VMEM((N_TABLE, 1, TOK), jnp.int32),
             pltpu.VMEM((N_TABLE, 1, TOK), jnp.int32),
             pltpu.VMEM((SLOTS, TOK), F32),
@@ -580,34 +644,44 @@
             pltpu.VMEM((PAIRS, 8, TOK), jnp.int32),
             pltpu.VMEM((PAIRS, TOK, 8), jnp.int32),
             buf(PAIRS, N_TABLE, 16, EMB), buf(PAIRS, N_TABLE, 16, EMB),
-            buf(PAIRS, N_TABLE, 16, EMB), buf(PAIRS, N_TABLE, 16, EMB),
-            buf(D, tokens), buf(D, tokens), buf(tokens, D), buf(tokens, PROJ),
-            buf(2, 4, 4, 256, 512), buf(4, 4, 256, 512),
-            buf(2, 2, 128, 512), buf(2, 2, 128, 512), buf(2, 4, 128, 512), buf(2, 4, 128, 512),
-            buf(4, 128, 512), buf(4, 128, 512),
-            buf(2, 64, 512), buf(2, 64, 512), buf(2, 128, 512), buf(2, 128, 512),
+            buf(PAIRS, N_TABLE, 16, EMB),
+            buf(D, tokens), buf(D, tokens), buf(tokens, PROJ),
+            buf(2, 4, 4, 256, 512), buf(4, 4, 256, 512), pltpu.VMEM((ROWS_DEV, EMB), F32),
+            buf(2, 2, CUT, 512), buf(2, 2, 256 - CUT, 512),
+            buf(2, 4, CUT, 512), buf(2, 4, 256 - CUT, 512),
+            buf(4, CUT, 512), buf(4, 256 - CUT, 512),
+            buf(2, CUT // 2, 512), buf(2, (256 - CUT) // 2, 512),
+            buf(2, CUT, 512), buf(2, 256 - CUT, 512),
             buf(8, 32, 512), buf(8, 32, 512),
-            buf(2, 4, 1024, 128), buf(4, 1024, 128), buf(2, 512, 128), buf(2, 1024, 128),
+            buf(4, 256, 512), buf(2, 256, 256), buf(2, 256, 512),
             dma((4,)), dma((8,)), dma((8,)), dma((32,)), dma((32,)),
             dma((PAIRS, 32)), dma((PAIRS, 32)), dma((PAIRS, 32)), dma((PAIRS, 32)),
-            dma((5,)), dma((5,)), dma((5, 6)), dma((5, 6)), dma((8,)), dma((8,)),
+            dma((8,)), dma((8,)), dma((5, 6)), dma((5, 6)), dma((8,)), dma((8,)),
         ],
         compiler_params=pltpu.CompilerParams(
             vmem_limit_bytes=VMEM_LIMIT, collective_id=0, has_side_effects=True
         ),
         name="whole_program",
-    )(message, order, table, upstream, proj_weight, out_weight)
+    )(*arrays)
+    return pl.pallas_call(
+        output_kernel,
+        out_shape=(
+            jax.ShapeDtypeStruct((32, 384), BF16),
+            jax.ShapeDtypeStruct((32, 128), BF16),
+            jax.ShapeDtypeStruct((64, 2048), BF16),
+        ),
+        in_specs=[whole] * 2,
+        out_specs=(whole,) * 3,
+        name="outputs",
+    )(*parts)
 
 
 def body(
     embed_table, owner_shard, slot_row, lengths, send_order, proj_weight, out_weight, upstream
 ):
-    ids = owner_shard[..., 0] * ROWS_DEV + slot_row
-    ids = jnp.swapaxes(ids, 1, 2).reshape(HIST, 2 * SEQ)
-    lengths = jnp.broadcast_to(lengths[:, None], (HIST, 2 * SEQ))
-    message = jnp.concatenate([ids, lengths], axis=1)
     proj, outw, table = run(
-        message, send_order.reshape(HIST, 1), embed_table, upstream.reshape(HIST * SEQ, D),
+        jnp.swapaxes(owner_shard[..., 0], 1, 2), jnp.swapaxes(slot_row, 1, 2),
+        lengths.reshape(1, HIST), send_order, embed_table, upstream.reshape(HIST * SEQ, D),
         proj_weight, out_weight,
     )
     return table.T, proj, outw

time: 162 us -> 151 us (0.932)
  local copies, waits for them, and re-layouts: 6.44 us -> 0 us
  Pallas kernels: 153 us -> 150 us
    unnamed x3 -> x0, local copies, waits for them, and re-layouts: 4.31 us -> none
    pallas_call x1 -> x2, Pallas kernels: 153 us -> 150 us  [the longest x1 149 us: run(): pl.pallas_call(program_kernel, out_shape=(jax.ShapeDtypeStruct((32, 512),...]
where the time goes in v3:
time: 151 us
  Pallas kernels  150 us (99%)
    pallas_call x1, Pallas kernels, run(): pl.pallas_call(program_kernel, out_shape=(jax.ShapeDtypeStruct((32, 512),...  149 us

profile of v3, /device:TPU:1, one launch (start us, length us, event | category | flops | bytes accessed | tf_op | source)
XLA Modules:
  0.0 151.1 jit_solution(9589023558585945201)
XLA Ops:
  0.6 148.7 %whole_program.1 = (bf16[32,512]{1,0:T(8,128)(2,1)}, bf16[256,512]{1,0:T(8,128)(2,1)}) custom-call(s32[8,2,64]{2,1,0:T(2,128)} %bitcast.8, s32[8,2,64]{2,1,0:T(2,128)} %bitcast.9, s32[1,8]{1,0:T(1,128)} %bitcast.10, s32[1,8]{1,0:T(1,128)} %order_ref.1, bf16[2048,512]{1,0:T(8,128)(2,1)} %table_hbm.1, bf16[512,1024]{1,0:T(8,128)(2,1)} %bitcast.7, ...), custom_call_target="tpu_custom_call" | custom-call | tf_op jit(solution)/shard_map/whole_program/pallas_call | solution.py:628
  149.3 1.8 %outputs.1 = (bf16[32,384]{1,0:T(8,128)(2,1)}, bf16[32,128]{1,0:T(8,128)(2,1)}, bf16[64,2048]{1,0:T(8,128)(2,1)}) custom-call(bf16[32,512]{1,0:T(8,128)(2,1)} %get-tuple-element.8.dense_ref, bf16[256,512]{1,0:T(8,128)(2,1)} %get-tuple-element.9.sums_ref), custom_call_target="tpu_custom_call" | custom-call | tf_op jit(solution)/shard_map/outputs/pallas_call | solution.py:666

commit v4 on v3

--- a/solution.py
+++ b/solution.py
@@ -424,22 +424,10 @@
             device_id=other, device_id_type=MESH,
         )
 
-    def terms(k, carry):
-        first = mm(normed_t[...], gbs[:, pl.ds(pl.multiple_of(k * 768, 768), 768)]) * SCALE
-        second = mm(mixed_t[...], up[:, pl.ds(pl.multiple_of(k * 256, 256), 256)]) * SCALE
-        for which, kept in ((0, 1 - c), (1, c)):
-            one = first[:, which * 384 : (which + 1) * 384].astype(BF16)
-            two = second[:, which * 128 : (which + 1) * 128].astype(BF16)
-            g[kept, k, :, :, 0:384] = one.reshape(4, 256, 384)
-            g[kept, k, :, :, 384:512] = two.reshape(4, 256, 128)
-        core_copy(k).start()
-        return carry
-
-    lax.fori_loop(0, 4, terms, 0)
     s1 = g.at[1]
     t2 = g.at[0]
 
-    def merge(k, carry):
+    def merge(k):
         core_copy(k).wait_recv()
         core_copy(k).wait_send()
 
@@ -448,9 +436,6 @@
             return inner
 
         lax.fori_loop(0, 4, step, 0)
-        return carry
-
-    lax.fori_loop(0, 4, merge, 0)
 
     def two(ref, n):
         return ref.at[pl.ds(2 * n, 2)]
@@ -485,13 +470,59 @@
                   ring_send.at[0], ring_recv.at[0])
     ring_b = Ring(x, x_right, x_left, lambda k: s1.at[:, k, pl.ds(CUT, 256 - CUT), :], two, far_b,
                   near_b, ring_send.at[1], ring_recv.at[1])
-    for ring in (ring_a, ring_b):
-        ring.make()
-        ring.start()
+    ring_a.make()
+
+    def chunk_at(n):
+        return lax.rem(y + 2 + n + (n // 2) * (1 - 2 * (n % 2)), 4)
+
+    def terms(n, carry):
+        k = chunk_at(n)
+        first = mm(normed_t[...], gbs[:, pl.ds(pl.multiple_of(k * 768, 768), 768)]) * SCALE
+        second = mm(mixed_t[...], up[:, pl.ds(pl.multiple_of(k * 256, 256), 256)]) * SCALE
+        for which, kept in ((0, 1 - c), (1, c)):
+            one = first[:, which * 384 : (which + 1) * 384].astype(BF16)
+            two_ = second[:, which * 128 : (which + 1) * 128].astype(BF16)
+            g[kept, k, :, :, 0:384] = one.reshape(4, 256, 384)
+            g[kept, k, :, :, 384:512] = two_.reshape(4, 256, 128)
+        core_copy(k).start()
+
+        @pl.when(n > 0)
+        def _():
+            merge(chunk_at(n - 1))
+
+        @pl.when(n == 1)
+        def _():
+            ring_a.copies[0].start()
+            ring_a.copies[1].start()
+
+        @pl.when(n == 2)
+        def _():
+            ring_a.copies[3].start()
+
+        @pl.when(n == 3)
+        def _():
+            ring_a.copies[2].start()
+
+        return carry
+
+    lax.fori_loop(0, 4, terms, 0)
+    merge(y)
+    ring_b.make()
+    ring_b.start()
     add_rows(0)
     ring_a.forward(add_into)
+    add_rows(1)
     ring_b.forward(add_into)
-    add_rows(1)
+    ring_a.arrive()
+    for n in range(4):
+        sum_a[n] = (
+            s1[y, n, 0:CUT, :].astype(F32) + near_a[0, n].astype(F32) + near_a[1, n].astype(F32)
+        ).astype(BF16)
+    ring_a2 = Ring(x, x_right, x_left, lambda k: sum_a.at[k],
+                   lambda ref, n: ref.at[pl.ds(CUT // 2 * n, CUT // 2), :], far_a2, near_a2,
+                   ring_send.at[2], ring_recv.at[2])
+    ring_a2.make()
+    ring_a2.start()
     ring_b.arrive()
     for n in range(4):
         sum_b[n] = (
@@ -502,25 +533,15 @@
                    far_b2, near_b2, ring_send.at[3], ring_recv.at[3])
     ring_b2.make()
     ring_b2.start()
-    ring_a.arrive()
-    for n in range(4):
-        sum_a[n] = (
-            s1[y, n, 0:CUT, :].astype(F32) + near_a[0, n].astype(F32) + near_a[1, n].astype(F32)
-        ).astype(BF16)
-    ring_a2 = Ring(x, x_right, x_left, lambda k: sum_a.at[k],
-                   lambda ref, n: ref.at[pl.ds(CUT // 2 * n, CUT // 2), :], far_a2, near_a2,
-                   ring_send.at[2], ring_recv.at[2])
-    ring_a2.make()
-    ring_a2.start()
+    ring_a2.forward(add_flat)
     ring_b2.forward(add_flat)
-    ring_a2.forward(add_flat)
     add_rows(2)
+    ring_a2.arrive()
+    total = sum_a[x].astype(F32) + near_a2[0].astype(F32) + near_a2[1].astype(F32)
+    s4[0 : CUT // 32] = total.astype(BF16).reshape(CUT // 32, 32, 512)
     ring_b2.arrive()
     total = sum_b[y].astype(F32) + near_b2[0].astype(F32) + near_b2[1].astype(F32)
     s4[CUT // 32 : 8] = total.astype(BF16).reshape(8 - CUT // 32, 32, 512)
-    ring_a2.arrive()
-    total = sum_a[x].astype(F32) + near_a2[0].astype(F32) + near_a2[1].astype(F32)
-    s4[0 : CUT // 32] = total.astype(BF16).reshape(CUT // 32, 32, 512)
 
     def z_copy(k):
         peer = lax.rem(z + k, 8)
@@ -579,13 +600,12 @@
     lax.fori_loop(2, 4, table_merge, 0)
     ring_t.start_half(1)
 
+    ring_t.forward(add_flat)
     total = s4[z].astype(F32)
     for k in range(1, 8):
         z_copy(k).wait_recv()
         total = total + zbuf[k].astype(F32)
     dense_ref[...] = total.astype(BF16)
-
-    ring_t.forward(add_flat)
     ring_t.arrive()
     total = t2[c, y].astype(F32) + t_near[0].astype(F32) + t_near[1].astype(F32)
     table_ref[...] = total.astype(BF16)

time: 151 us -> 151 us (level)
  no operation moved by 1% of the time
where the time goes in v4:
time: 151 us
  Pallas kernels  150 us (99%)
    pallas_call x1, Pallas kernels, run(): pl.pallas_call(program_kernel, out_shape=(jax.ShapeDtypeStruct((32, 512),...  148 us

profile of v4, /device:TPU:1, one launch (start us, length us, event | category | flops | bytes accessed | tf_op | source)
XLA Modules:
  0.0 150.9 jit_solution(14730755589375689159)
XLA Ops:
  0.6 148.4 %whole_program.1 = (bf16[32,512]{1,0:T(8,128)(2,1)}, bf16[256,512]{1,0:T(8,128)(2,1)}) custom-call(s32[8,2,64]{2,1,0:T(2,128)} %bitcast.8, s32[8,2,64]{2,1,0:T(2,128)} %bitcast.9, s32[1,8]{1,0:T(1,128)} %bitcast.10, s32[1,8]{1,0:T(1,128)} %order_ref.1, bf16[2048,512]{1,0:T(8,128)(2,1)} %table_hbm.1, bf16[512,1024]{1,0:T(8,128)(2,1)} %bitcast.7, ...), custom_call_target="tpu_custom_call" | custom-call | tf_op jit(solution)/shard_map/whole_program/pallas_call | solution.py:648
  149.1 1.8 %outputs.1 = (bf16[32,384]{1,0:T(8,128)(2,1)}, bf16[32,128]{1,0:T(8,128)(2,1)}, bf16[64,2048]{1,0:T(8,128)(2,1)}) custom-call(bf16[32,512]{1,0:T(8,128)(2,1)} %get-tuple-element.8.dense_ref, bf16[256,512]{1,0:T(8,128)(2,1)} %get-tuple-element.9.sums_ref), custom_call_target="tpu_custom_call" | custom-call | tf_op jit(solution)/shard_map/outputs/pallas_call | solution.py:686

commit v5 on v4

--- a/solution.py
+++ b/solution.py
@@ -25,7 +25,7 @@
 SCALE = float(2048 * 64) ** (-0.5)
 MESH = pl.DeviceIdType.MESH
 VMEM_LIMIT = 60 * 1024 * 1024
-CUT = 160
+STREAMS = ((0, 96, True), (96, 96, True), (192, 64, False))
 F32 = jnp.float32
 BF16 = jnp.bfloat16
 
@@ -196,8 +196,9 @@
     dense_ref, table_ref,
     table, up, wp, wo, msg_out, msg_in, req_out, req_in, wanted, req_rows, rows_s, cols_s,
     picked, replies, incoming, normed_t, mixed_t, gbs,
-    g, core_buf, sums, far_a, far_b, near_a, near_b, sum_a, sum_b,
-    far_a2, far_b2, near_a2, near_b2, s4, zbuf, t_core, t_far, t_near,
+    g, core_buf, sums, far_1, far_2, far_3, near_1, near_2, near_3, sum_1, sum_2, sum_3,
+    last_far_1, last_far_2, last_far_3, last_near_1, last_near_2, last_near_3,
+    s4, zbuf, t_core, t_far, t_near,
     load_sem, m_send, m_recv, r_send, r_recv, f_send, f_recv, a_send, a_recv,
     core_send, core_recv, ring_send, ring_recv, z_send, z_recv,
 ):
@@ -466,11 +467,63 @@
 
         lax.fori_loop(0, 4, block, 0)
 
-    ring_a = Ring(y, y_right, y_left, lambda k: s1.at[k, :, pl.ds(0, CUT), :], two, far_a, near_a,
-                  ring_send.at[0], ring_recv.at[0])
-    ring_b = Ring(x, x_right, x_left, lambda k: s1.at[:, k, pl.ds(CUT, 256 - CUT), :], two, far_b,
-                  near_b, ring_send.at[1], ring_recv.at[1])
-    ring_a.make()
+    fars, nears, partials = (far_1, far_2, far_3), (near_1, near_2, near_3), (sum_1, sum_2, sum_3)
+    last_fars = (last_far_1, last_far_2, last_far_3)
+    last_nears = (last_near_1, last_near_2, last_near_3)
+
+    def ring_on(over_y, chunk, half, far, near, number):
+        place, right, left = (y, y_right, y_left) if over_y else (x, x_right, x_left)
+        ring = Ring(place, right, left, chunk, half, far, near,
+                    ring_send.at[number], ring_recv.at[number])
+        ring.make()
+        return ring
+
+    def first_chunk(n):
+        first, count, over_y = STREAMS[n]
+        if over_y:
+            return lambda k: s1.at[k, :, pl.ds(first, count), :]
+        return lambda k: s1.at[:, k, pl.ds(first, count), :]
+
+    def half_rows(count):
+        return lambda ref, n: ref.at[pl.ds(count // 2 * n, count // 2), :]
+
+    firsts = [
+        ring_on(STREAMS[n][2], first_chunk(n), two, fars[n], nears[n], n) for n in range(3)
+    ]
+    seconds = [
+        ring_on(not STREAMS[n][2], lambda k, n=n: partials[n].at[k], half_rows(STREAMS[n][1]),
+                last_fars[n], last_nears[n], 3 + n)
+        for n in range(3)
+    ]
+
+    def turn(n):
+        first, count, over_y = STREAMS[n]
+        firsts[n].arrive()
+        for m in range(4):
+            own = s1[y, m, first : first + count, :] if over_y else s1[m, x, first : first + count, :]
+            total = own.astype(F32) + nears[n][0, m].astype(F32) + nears[n][1, m].astype(F32)
+            partials[n][m] = total.astype(BF16)
+        seconds[n].start()
+
+    def z_copy(target, source):
+        return pltpu.make_async_remote_copy(
+            src_ref=s4.at[target], dst_ref=zbuf.at[source],
+            send_sem=z_send.at[target], recv_sem=z_recv.at[source],
+            device_id=(dp, 8 * x + target), device_id_type=MESH,
+        )
+
+    def leave(n):
+        first, count, over_y = STREAMS[n]
+        seconds[n].arrive()
+        place = x if over_y else y
+        total = partials[n][place].astype(F32) + last_nears[n][0].astype(F32)
+        total = (total + last_nears[n][1].astype(F32)).astype(BF16)
+        s4[first // 32 : (first + count) // 32] = total.reshape(count // 32, 32, 512)
+        for target in range(first // 32, (first + count) // 32):
+
+            @pl.when(z != target)
+            def _():
+                z_copy(target, z).start()
 
     def chunk_at(n):
         return lax.rem(y + 2 + n + (n // 2) * (1 - 2 * (n % 2)), 4)
@@ -492,67 +545,41 @@
 
         @pl.when(n == 1)
         def _():
-            ring_a.copies[0].start()
-            ring_a.copies[1].start()
+            firsts[0].copies[0].start()
+            firsts[0].copies[1].start()
 
         @pl.when(n == 2)
         def _():
-            ring_a.copies[3].start()
+            firsts[0].copies[3].start()
 
         @pl.when(n == 3)
         def _():
-            ring_a.copies[2].start()
+            firsts[0].copies[2].start()
 
         return carry
 
     lax.fori_loop(0, 4, terms, 0)
     merge(y)
-    ring_b.make()
-    ring_b.start()
+    firsts[2].start()
+    firsts[1].copies[0].start()
+    firsts[1].copies[1].start()
     add_rows(0)
-    ring_a.forward(add_into)
+    firsts[0].forward(add_into)
+    firsts[1].copies[2].start()
+    firsts[1].copies[3].start()
+    turn(0)
+    firsts[1].forward(add_into)
     add_rows(1)
-    ring_b.forward(add_into)
-    ring_a.arrive()
-    for n in range(4):
-        sum_a[n] = (
-            s1[y, n, 0:CUT, :].astype(F32) + near_a[0, n].astype(F32) + near_a[1, n].astype(F32)
-        ).astype(BF16)
-    ring_a2 = Ring(x, x_right, x_left, lambda k: sum_a.at[k],
-                   lambda ref, n: ref.at[pl.ds(CUT // 2 * n, CUT // 2), :], far_a2, near_a2,
-                   ring_send.at[2], ring_recv.at[2])
-    ring_a2.make()
-    ring_a2.start()
-    ring_b.arrive()
-    for n in range(4):
-        sum_b[n] = (
-            s1[n, x, CUT:256, :].astype(F32) + near_b[0, n].astype(F32) + near_b[1, n].astype(F32)
-        ).astype(BF16)
-    ring_b2 = Ring(y, y_right, y_left, lambda k: sum_b.at[k],
-                   lambda ref, n: ref.at[pl.ds((256 - CUT) // 2 * n, (256 - CUT) // 2), :],
-                   far_b2, near_b2, ring_send.at[3], ring_recv.at[3])
-    ring_b2.make()
-    ring_b2.start()
-    ring_a2.forward(add_flat)
-    ring_b2.forward(add_flat)
+    firsts[2].forward(add_into)
+    seconds[0].forward(add_flat)
+    turn(1)
+    turn(2)
+    leave(0)
     add_rows(2)
-    ring_a2.arrive()
-    total = sum_a[x].astype(F32) + near_a2[0].astype(F32) + near_a2[1].astype(F32)
-    s4[0 : CUT // 32] = total.astype(BF16).reshape(CUT // 32, 32, 512)
-    ring_b2.arrive()
-    total = sum_b[y].astype(F32) + near_b2[0].astype(F32) + near_b2[1].astype(F32)
-    s4[CUT // 32 : 8] = total.astype(BF16).reshape(8 - CUT // 32, 32, 512)
-
-    def z_copy(k):
-        peer = lax.rem(z + k, 8)
-        return pltpu.make_async_remote_copy(
-            src_ref=s4.at[peer], dst_ref=zbuf.at[k],
-            send_sem=z_send.at[k], recv_sem=z_recv.at[k],
-            device_id=(dp, 8 * x + peer), device_id_type=MESH,
-        )
-
-    for k in range(1, 8):
-        z_copy(k).start()
+    seconds[1].forward(add_flat)
+    seconds[2].forward(add_flat)
+    leave(1)
+    leave(2)
 
     take_in(PAIRS - 1)
 
@@ -591,7 +618,7 @@
 
     ring_t = Ring(y, y_right, y_left, lambda k: t2.at[c, k],
                   lambda ref, n: ref.at[:, pl.ds(256 * n, 256)], t_far, t_near,
-                  ring_send.at[4], ring_recv.at[4])
+                  ring_send.at[6], ring_recv.at[6])
     ring_t.make()
     lax.fori_loop(0, 3, table_block, 0)
     lax.fori_loop(0, 2, table_merge, 0)
@@ -603,8 +630,9 @@
     ring_t.forward(add_flat)
     total = s4[z].astype(F32)
     for k in range(1, 8):
-        z_copy(k).wait_recv()
-        total = total + zbuf[k].astype(F32)
+        source = lax.rem(z + k, 8)
+        z_copy(z, source).wait_recv()
+        total = total + zbuf[source].astype(F32)
     dense_ref[...] = total.astype(BF16)
     ring_t.arrive()
     total = t2[c, y].astype(F32) + t_near[0].astype(F32) + t_near[1].astype(F32)
@@ -621,8 +649,8 @@
         t_copy(k).wait_send()
     for k in range(1, 8):
         msg_copy(k).wait_send()
-        z_copy(k).wait_send()
-    for ring in (ring_a, ring_b, ring_a2, ring_b2, ring_t):
+        z_copy(lax.rem(z + k, 8), z).wait_send()
+    for ring in (*firsts, *seconds, ring_t):
         ring.end()
 
 
@@ -667,16 +695,16 @@
             buf(PAIRS, N_TABLE, 16, EMB),
             buf(D, tokens), buf(D, tokens), buf(tokens, PROJ),
             buf(2, 4, 4, 256, 512), buf(4, 4, 256, 512), pltpu.VMEM((ROWS_DEV, EMB), F32),
-            buf(2, 2, CUT, 512), buf(2, 2, 256 - CUT, 512),
-            buf(2, 4, CUT, 512), buf(2, 4, 256 - CUT, 512),
-            buf(4, CUT, 512), buf(4, 256 - CUT, 512),
-            buf(2, CUT // 2, 512), buf(2, (256 - CUT) // 2, 512),
-            buf(2, CUT, 512), buf(2, 256 - CUT, 512),
+            *[buf(2, 2, n, 512) for _, n, _ in STREAMS],
+            *[buf(2, 4, n, 512) for _, n, _ in STREAMS],
+            *[buf(4, n, 512) for _, n, _ in STREAMS],
+            *[buf(2, n // 2, 512) for _, n, _ in STREAMS],
+            *[buf(2, n, 512) for _, n, _ in STREAMS],
             buf(8, 32, 512), buf(8, 32, 512),
             buf(4, 256, 512), buf(2, 256, 256), buf(2, 256, 512),
             dma((4,)), dma((8,)), dma((8,)), dma((32,)), dma((32,)),
             dma((PAIRS, 32)), dma((PAIRS, 32)), dma((PAIRS, 32)), dma((PAIRS, 32)),
-            dma((8,)), dma((8,)), dma((5, 6)), dma((5, 6)), dma((8,)), dma((8,)),
+            dma((8,)), dma((8,)), dma((7, 6)), dma((7, 6)), dma((8,)), dma((8,)),
         ],
         compiler_params=pltpu.CompilerParams(
             vmem_limit_bytes=VMEM_LIMIT, collective_id=0, has_side_effects=True

time: 151 us -> 149 us (0.987)
  Pallas kernels: 150 us -> 148 us
    pallas_call x1, Pallas kernels: 148 us -> 147 us  [run(): pl.pallas_call(program_kernel, out_shape=(jax.ShapeDtypeStruct((32, 512),...]
where the time goes in v5:
time: 149 us
  Pallas kernels  148 us (99%)
    pallas_call x1, Pallas kernels, run(): pl.pallas_call(program_kernel, out_shape=(jax.ShapeDtypeStruct((32, 512),...  147 us

profile of v5, /device:TPU:1, one launch (start us, length us, event | category | flops | bytes accessed | tf_op | source)
XLA Modules:
  0.0 149.1 jit_solution(8484766628829961334)
XLA Ops:
  0.6 146.6 %whole_program.1 = (bf16[32,512]{1,0:T(8,128)(2,1)}, bf16[256,512]{1,0:T(8,128)(2,1)}) custom-call(s32[8,2,64]{2,1,0:T(2,128)} %bitcast.8, s32[8,2,64]{2,1,0:T(2,128)} %bitcast.9, s32[1,8]{1,0:T(1,128)} %bitcast.10, s32[1,8]{1,0:T(1,128)} %order_ref.1, bf16[2048,512]{1,0:T(8,128)(2,1)} %table_hbm.1, bf16[512,1024]{1,0:T(8,128)(2,1)} %bitcast.7, ...), custom_call_target="tpu_custom_call" | custom-call | tf_op jit(solution)/shard_map/whole_program/pallas_call | solution.py:676
  147.2 1.8 %outputs.1 = (bf16[32,384]{1,0:T(8,128)(2,1)}, bf16[32,128]{1,0:T(8,128)(2,1)}, bf16[64,2048]{1,0:T(8,128)(2,1)}) custom-call(bf16[32,512]{1,0:T(8,128)(2,1)} %get-tuple-element.8.dense_ref, bf16[256,512]{1,0:T(8,128)(2,1)} %get-tuple-element.9.sums_ref), custom_call_target="tpu_custom_call" | custom-call | tf_op jit(solution)/shard_map/outputs/pallas_call | solution.py:714

commit v6 on v5

--- a/solution.py
+++ b/solution.py
@@ -373,20 +373,24 @@
 
     outgoing = picked
 
-    def give_copy(p, k):
+    def give_copy(last, k):
         peer = lax.rem(tab + k, 32)
+        pairs = pl.ds(PAIRS - 1, 1) if last else pl.ds(0, PAIRS - 1)
         return pltpu.make_async_remote_copy(
-            src_ref=outgoing.at[p, peer], dst_ref=incoming.at[p, tab],
-            send_sem=a_send.at[p, k], recv_sem=a_recv.at[p, k],
+            src_ref=outgoing.at[pairs, peer], dst_ref=incoming.at[pairs, tab],
+            send_sem=a_send.at[last, k], recv_sem=a_recv.at[last, k],
             device_id=(dp, peer), device_id_type=MESH,
         )
 
     for load in loads[1:]:
         load.wait()
 
-    def give(n, carry):
-        give_copy(n // 31, n % 31 + 1).start()
-        return carry
+    def give(last):
+        def start(k, carry):
+            give_copy(last, k).start()
+            return carry
+
+        lax.fori_loop(1, 32, start, 0)
 
     def fetched(p):
         def landed(k, carry):
@@ -401,7 +405,7 @@
 
         @pl.when(p == PAIRS - 1)
         def _():
-            lax.fori_loop(0, (PAIRS - 1) * 31, give, 0)
+            give(0)
 
         tokens = pl.ds(pl.multiple_of(p * TOK, TOK), TOK)
         normed_p, mixed_p, top_p, before_p, back = layer_pair(
@@ -416,7 +420,6 @@
         return carry
 
     lax.fori_loop(0, PAIRS, pair, 0)
-    lax.fori_loop((PAIRS - 1) * 31, PAIRS * 31, give, 0)
 
     def core_copy(k):
         return pltpu.make_async_remote_copy(
@@ -444,28 +447,30 @@
     def add_flat(target, other_ref):
         target[...] = (target[...].astype(F32) + other_ref[...].astype(F32)).astype(BF16)
 
-    def chosen_rows(p, first, count):
-        places = lax.broadcasted_iota(jnp.int32, (count, SLOTS), 0) + first
-        return (places == req_rows[:, p * SLOTS : (p + 1) * SLOTS]).astype(BF16)
-
-    def take_in(p):
+    def chosen_rows(slots, first, count):
+        asked_row = req_rows[:, slots]
+        places = lax.broadcasted_iota(jnp.int32, (count, asked_row.shape[1]), 0) + first
+        return (places == asked_row).astype(BF16)
+
+    def take_in(last):
         def given(k, carry):
-            give_copy(p, k).wait_recv()
+            give_copy(last, k).wait_recv()
             return carry
 
         lax.fori_loop(1, 32, given, 0)
 
-    def add_rows(p):
-        take_in(p)
+    early = (PAIRS - 1) * SLOTS
+
+    def add_rows():
+        take_in(0)
 
         def block(b, carry):
-            first = b * 512
-            part = mm(chosen_rows(p, first, 512), incoming[p].reshape(SLOTS, EMB))
-            rows = pl.ds(pl.multiple_of(first, 512), 512)
-            sums[rows, :] = part if p == 0 else sums[rows, :] + part
+            rows = pl.ds(pl.multiple_of(b * 256, 256), 256)
+            rows_in = incoming[0 : PAIRS - 1].reshape(early, EMB)
+            sums[rows, :] = mm(chosen_rows(slice(0, early), b * 256, 256), rows_in)
             return carry
 
-        lax.fori_loop(0, 4, block, 0)
+        lax.fori_loop(0, 8, block, 0)
 
     fars, nears, partials = (far_1, far_2, far_3), (near_1, near_2, near_3), (sum_1, sum_2, sum_3)
     last_fars = (last_far_1, last_far_2, last_far_3)
@@ -563,28 +568,27 @@
     firsts[2].start()
     firsts[1].copies[0].start()
     firsts[1].copies[1].start()
-    add_rows(0)
+    give(1)
     firsts[0].forward(add_into)
     firsts[1].copies[2].start()
     firsts[1].copies[3].start()
     turn(0)
     firsts[1].forward(add_into)
-    add_rows(1)
     firsts[2].forward(add_into)
     seconds[0].forward(add_flat)
+    add_rows()
     turn(1)
     turn(2)
     leave(0)
-    add_rows(2)
     seconds[1].forward(add_flat)
     seconds[2].forward(add_flat)
     leave(1)
     leave(2)
 
-    take_in(PAIRS - 1)
+    take_in(1)
 
     def rows_of(first):
-        part = mm(chosen_rows(PAIRS - 1, first, 256), incoming[PAIRS - 1].reshape(SLOTS, EMB))
+        part = mm(chosen_rows(slice(early, early + SLOTS), first, 256), incoming[PAIRS - 1].reshape(SLOTS, EMB))
         rows = pl.ds(pl.multiple_of(first, 256), 256)
         return (sums[rows, :] + part).astype(BF16).astype(F32)
 
@@ -640,8 +644,8 @@
 
     def sent(k, carry):
         req_copy(k).wait_send()
-        for p in range(PAIRS):
-            give_copy(p, k).wait_send()
+        give_copy(0, k).wait_send()
+        give_copy(1, k).wait_send()
         return carry
 
     lax.fori_loop(1, 32, sent, 0)
@@ -703,7 +707,7 @@
             buf(8, 32, 512), buf(8, 32, 512),
             buf(4, 256, 512), buf(2, 256, 256), buf(2, 256, 512),
             dma((4,)), dma((8,)), dma((8,)), dma((32,)), dma((32,)),
-            dma((PAIRS, 32)), dma((PAIRS, 32)), dma((PAIRS, 32)), dma((PAIRS, 32)),
+            dma((PAIRS, 32)), dma((PAIRS, 32)), dma((2, 32)), dma((2, 32)),
             dma((8,)), dma((8,)), dma((7, 6)), dma((7, 6)), dma((8,)), dma((8,)),
         ],
         compiler_params=pltpu.CompilerParams(

time: 149 us -> 146 us (0.980)
  Pallas kernels: 148 us -> 145 us
    pallas_call x1, Pallas kernels: 147 us -> 143 us  [run(): pl.pallas_call(program_kernel, out_shape=(jax.ShapeDtypeStruct((32, 512),...]
where the time goes in v6:
time: 146 us; the launch traced here: 145 us
  Pallas kernels  145 us (99%)
    pallas_call x1, Pallas kernels, run(): pl.pallas_call(program_kernel, out_shape=(jax.ShapeDtypeStruct((32, 512),...  143 us

profile of v6, /device:TPU:1, one launch (start us, length us, event | category | flops | bytes accessed | tf_op | source)
XLA Modules:
  0.0 145.4 jit_solution(11104837136308494557)
XLA Ops:
  0.6 143.0 %whole_program.1 = (bf16[32,512]{1,0:T(8,128)(2,1)}, bf16[256,512]{1,0:T(8,128)(2,1)}) custom-call(s32[8,2,64]{2,1,0:T(2,128)} %bitcast.8, s32[8,2,64]{2,1,0:T(2,128)} %bitcast.9, s32[1,8]{1,0:T(1,128)} %bitcast.10, s32[1,8]{1,0:T(1,128)} %order_ref.1, bf16[2048,512]{1,0:T(8,128)(2,1)} %table_hbm.1, bf16[512,1024]{1,0:T(8,128)(2,1)} %bitcast.7, ...), custom_call_target="tpu_custom_call" | custom-call | tf_op jit(solution)/shard_map/whole_program/pallas_call | solution.py:680
  143.6 1.8 %outputs.1 = (bf16[32,384]{1,0:T(8,128)(2,1)}, bf16[32,128]{1,0:T(8,128)(2,1)}, bf16[64,2048]{1,0:T(8,128)(2,1)}) custom-call(bf16[32,512]{1,0:T(8,128)(2,1)} %get-tuple-element.8.dense_ref, bf16[256,512]{1,0:T(8,128)(2,1)} %get-tuple-element.9.sums_ref), custom_call_target="tpu_custom_call" | custom-call | tf_op jit(solution)/shard_map/outputs/pallas_call | solution.py:718

commit v7 on v6

--- a/solution.py
+++ b/solution.py
@@ -582,8 +582,6 @@
     leave(0)
     seconds[1].forward(add_flat)
     seconds[2].forward(add_flat)
-    leave(1)
-    leave(2)
 
     take_in(1)
 
@@ -630,8 +628,18 @@
     lax.fori_loop(3, 4, table_block, 0)
     lax.fori_loop(2, 4, table_merge, 0)
     ring_t.start_half(1)
+    leave(1)
+    leave(2)
 
     ring_t.forward(add_flat)
+
+    def sent(k, carry):
+        req_copy(k).wait_send()
+        give_copy(0, k).wait_send()
+        give_copy(1, k).wait_send()
+        return carry
+
+    lax.fori_loop(1, 32, sent, 0)
     total = s4[z].astype(F32)
     for k in range(1, 8):
         source = lax.rem(z + k, 8)
@@ -642,13 +650,6 @@
     total = t2[c, y].astype(F32) + t_near[0].astype(F32) + t_near[1].astype(F32)
     table_ref[...] = total.astype(BF16)
 
-    def sent(k, carry):
-        req_copy(k).wait_send()
-        give_copy(0, k).wait_send()
-        give_copy(1, k).wait_send()
-        return carry
-
-    lax.fori_loop(1, 32, sent, 0)
     for k in range(4):
         t_copy(k).wait_send()
     for k in range(1, 8):

time: 146 us -> 143 us (0.979)
  Pallas kernels: 145 us -> 142 us
    pallas_call x1, Pallas kernels: 143 us -> 140 us  [run(): pl.pallas_call(program_kernel, out_shape=(jax.ShapeDtypeStruct((32, 512),...]
where the time goes in v7:
time: 143 us
  Pallas kernels  142 us (99%)
    pallas_call x1, Pallas kernels, run(): pl.pallas_call(program_kernel, out_shape=(jax.ShapeDtypeStruct((32, 512),...  140 us

profile of v7, /device:TPU:1, one launch (start us, length us, event | category | flops | bytes accessed | tf_op | source)
XLA Modules:
  0.0 142.9 jit_solution(8988597245088434752)
XLA Ops:
  0.6 140.4 %whole_program.1 = (bf16[32,512]{1,0:T(8,128)(2,1)}, bf16[256,512]{1,0:T(8,128)(2,1)}) custom-call(s32[8,2,64]{2,1,0:T(2,128)} %bitcast.8, s32[8,2,64]{2,1,0:T(2,128)} %bitcast.9, s32[1,8]{1,0:T(1,128)} %bitcast.10, s32[1,8]{1,0:T(1,128)} %order_ref.1, bf16[2048,512]{1,0:T(8,128)(2,1)} %table_hbm.1, bf16[512,1024]{1,0:T(8,128)(2,1)} %bitcast.7, ...), custom_call_target="tpu_custom_call" | custom-call | tf_op jit(solution)/shard_map/whole_program/pallas_call | solution.py:681
  141.1 1.8 %outputs.1 = (bf16[32,384]{1,0:T(8,128)(2,1)}, bf16[32,128]{1,0:T(8,128)(2,1)}, bf16[64,2048]{1,0:T(8,128)(2,1)}) custom-call(bf16[32,512]{1,0:T(8,128)(2,1)} %get-tuple-element.8.dense_ref, bf16[256,512]{1,0:T(8,128)(2,1)} %get-tuple-element.9.sums_ref), custom_call_target="tpu_custom_call" | custom-call | tf_op jit(solution)/shard_map/outputs/pallas_call | solution.py:719

commit v8 on v7

--- a/solution.py
+++ b/solution.py
@@ -304,11 +304,14 @@
             device_id=(dp, peer), device_id_type=MESH,
         )
 
-    def ask(k, carry):
-        req_copy(k).start()
-        return carry
-
-    lax.fori_loop(1, 32, ask, 0)
+    def zigzag(n):
+        return (1 - n % 2) * (n // 2 + 1) + n % 2 * (31 - n // 2)
+
+    def ask(n, carry):
+        req_copy(zigzag(n)).start()
+        return carry
+
+    lax.fori_loop(0, 31, ask, 0)
     req_in[tab] = req_out[tab]
 
     slot = owner * 16 + rank.astype(jnp.int32)
@@ -361,11 +364,11 @@
         chosen = (places == line).astype(BF16)
         picked[p] = mm(chosen, table[...]).astype(BF16).reshape(N_TABLE, 16, EMB)
 
-        def start(k, inner):
-            fetch_copy(p, k).start()
+        def start(n, inner):
+            fetch_copy(p, zigzag(n)).start()
             return inner
 
-        lax.fori_loop(1, 32, start, 0)
+        lax.fori_loop(0, 31, start, 0)
         replies[p, tab] = picked[p, tab]
         return carry
 
@@ -386,11 +389,11 @@
         load.wait()
 
     def give(last):
-        def start(k, carry):
-            give_copy(last, k).start()
+        def start(n, carry):
+            give_copy(last, zigzag(n)).start()
             return carry
 
-        lax.fori_loop(1, 32, start, 0)
+        lax.fori_loop(0, 31, start, 0)
 
     def fetched(p):
         def landed(k, carry):

time: 143 us -> 150 us (1.049)
  Pallas kernels: 142 us -> 149 us
    pallas_call x1, Pallas kernels: 140 us -> 147 us  [run(): pl.pallas_call(program_kernel, out_shape=(jax.ShapeDtypeStruct((32, 512),...]
where the time goes in v8:
time: 150 us
  Pallas kernels  149 us (99%)
    pallas_call x1, Pallas kernels, run(): pl.pallas_call(program_kernel, out_shape=(jax.ShapeDtypeStruct((32, 512),...  147 us

profile of v8, /device:TPU:1, one launch (start us, length us, event | category | flops | bytes accessed | tf_op | source)
XLA Modules:
  0.0 149.8 jit_solution(6817583562551184050)
XLA Ops:
  0.6 147.3 %whole_program.1 = (bf16[32,512]{1,0:T(8,128)(2,1)}, bf16[256,512]{1,0:T(8,128)(2,1)}) custom-call(s32[8,2,64]{2,1,0:T(2,128)} %bitcast.8, s32[8,2,64]{2,1,0:T(2,128)} %bitcast.9, s32[1,8]{1,0:T(1,128)} %bitcast.10, s32[1,8]{1,0:T(1,128)} %order_ref.1, bf16[2048,512]{1,0:T(8,128)(2,1)} %table_hbm.1, bf16[512,1024]{1,0:T(8,128)(2,1)} %bitcast.7, ...), custom_call_target="tpu_custom_call" | custom-call | tf_op jit(solution)/shard_map/whole_program/pallas_call | solution.py:684
  148.0 1.8 %outputs.1 = (bf16[32,384]{1,0:T(8,128)(2,1)}, bf16[32,128]{1,0:T(8,128)(2,1)}, bf16[64,2048]{1,0:T(8,128)(2,1)}) custom-call(bf16[32,512]{1,0:T(8,128)(2,1)} %get-tuple-element.8.dense_ref, bf16[256,512]{1,0:T(8,128)(2,1)} %get-tuple-element.9.sums_ref), custom_call_target="tpu_custom_call" | custom-call | tf_op jit(solution)/shard_map/outputs/pallas_call | solution.py:722

commit v9 on v7

--- a/solution.py
+++ b/solution.py
@@ -374,7 +374,7 @@
     outgoing = picked
 
     def give_copy(last, k):
-        peer = lax.rem(tab + k, 32)
+        peer = 8 * lax.rem(x + k // 8, 4) + lax.rem(z + k % 8, 8)
         pairs = pl.ds(PAIRS - 1, 1) if last else pl.ds(0, PAIRS - 1)
         return pltpu.make_async_remote_copy(
             src_ref=outgoing.at[pairs, peer], dst_ref=incoming.at[pairs, tab],
@@ -386,11 +386,11 @@
         load.wait()
 
     def give(last):
-        def start(k, carry):
-            give_copy(last, k).start()
+        def start(n, carry):
+            give_copy(last, 31 - n).start()
             return carry
 
-        lax.fori_loop(1, 32, start, 0)
+        lax.fori_loop(0, 31, start, 0)
 
     def fetched(p):
         def landed(k, carry):

time: 143 us -> 143 us (level)
  no operation moved by 1% of the time
where the time goes in v9:
time: 143 us
  Pallas kernels  142 us (99%)
    pallas_call x1, Pallas kernels, run(): pl.pallas_call(program_kernel, out_shape=(jax.ShapeDtypeStruct((32, 512),...  140 us

profile of v9, /device:TPU:1, one launch (start us, length us, event | category | flops | bytes accessed | tf_op | source)
XLA Modules:
  0.0 142.6 jit_solution(4866719726868686127)
XLA Ops:
  0.6 140.2 %whole_program.1 = (bf16[32,512]{1,0:T(8,128)(2,1)}, bf16[256,512]{1,0:T(8,128)(2,1)}) custom-call(s32[8,2,64]{2,1,0:T(2,128)} %bitcast.8, s32[8,2,64]{2,1,0:T(2,128)} %bitcast.9, s32[1,8]{1,0:T(1,128)} %bitcast.10, s32[1,8]{1,0:T(1,128)} %order_ref.1, bf16[2048,512]{1,0:T(8,128)(2,1)} %table_hbm.1, bf16[512,1024]{1,0:T(8,128)(2,1)} %bitcast.7, ...), custom_call_target="tpu_custom_call" | custom-call | tf_op jit(solution)/shard_map/whole_program/pallas_call | solution.py:681
  140.8 1.8 %outputs.1 = (bf16[32,384]{1,0:T(8,128)(2,1)}, bf16[32,128]{1,0:T(8,128)(2,1)}, bf16[64,2048]{1,0:T(8,128)(2,1)}) custom-call(bf16[32,512]{1,0:T(8,128)(2,1)} %get-tuple-element.8.dense_ref, bf16[256,512]{1,0:T(8,128)(2,1)} %get-tuple-element.9.sums_ref), custom_call_target="tpu_custom_call" | custom-call | tf_op jit(solution)/shard_map/outputs/pallas_call | solution.py:719
